TPU v7x, 32 devices: a whole 2x2x4 slice. The times are simulated.
32 devices in a mesh: grp: 2 (over y), blk: 4 (over z), head: 4 (over x, core).
Axes of the slice: x: 2, y: 2, z: 4, core: 2. Of those that a mesh axis runs over, the one named last changes fastest.
Arguments:
- query: bfloat16 [2048, 512], P(('grp', 'blk', 'head')), parts along dimension 0, may hold values from -128 to 128
- keys: bfloat16 [2048, 512], P(('grp', 'blk', 'head')), parts along dimension 0, may hold values from -8 to 8
- values: bfloat16 [2048, 512], P(('grp', 'blk', 'head')), parts along dimension 0, may hold values from -6 to 6
- grad_out: bfloat16 [2048, 512], P(('grp', 'blk', 'head')), parts along dimension 0, may hold values from -6 to 6
- valid: int32 [64], P('grp'), parts along dimension 0, may hold values from 16 to 32, as said below
- views: int32 [64], P('grp'), parts along dimension 0, may hold values from 0 to 1
- cross_bias: float32 [8], replicated, may hold values from -2 to 2
Outputs:
- grad_query: float32 [2048, 512], P(('grp', 'blk', 'head')), parts along dimension 0
- grad_keys: float32 [2048, 512], P(('grp', 'blk', 'head')), parts along dimension 0
- grad_values: float32 [2048, 512], P(('grp', 'blk', 'head')), parts along dimension 0
There are 2 independent parts, one for each index of `grp`. A program takes and returns all parts, laid end to end along the dimension named above; an argument that names none is the same for every part. Nothing has to cross between parts.
Inputs may be any that keep to these rules, and one draw needn't show every extreme that they name: `valid`: every frame has at least half of its slots live, and some frame has all 32 live.
All inputs are finite; a program needn't handle non-finite values.
Results may differ from a plain program's by a relative error of at most 0.025.
Values may be sent and summed in bfloat16 or wider, within the bound.
No kernel may reach another device: no remote copies, remote signals or barrier semaphores. Data moves between devices by JAX's collectives and lax.ppermute only.
A program may use at most 64 MiB of HBM per device.

v0:
```python
import functools
import math

import jax
import jax.numpy as jnp
from jax import lax
from jax.experimental import pallas as pl
from jax.experimental.pallas import tpu as pltpu
from jax.sharding import Mesh, PartitionSpec as P

HD = 64
FRAME = 32
PAIR = 2 * HD
TILE = 128
CHUNK = 128
UNROLL = 2

SCALE = 0.125
DEAD = -1e30
LOG2E = math.log2(math.e)
LIMIT = 48 * 1024 * 1024

VMEM = pl.BlockSpec(memory_space=pltpu.VMEM)
SMEM = pl.BlockSpec(memory_space=pltpu.SMEM)


def side_by_side(left, right):
    return jnp.concatenate([left, right], axis=1)


def pack_kernel(q_ref, k_ref, v_ref, g_ref, out_ref):
    rows, width = q_ref.shape
    q, k, v, g = q_ref[...], k_ref[...], v_ref[...], g_ref[...]
    for head in range(width // HD):
        at = slice(head * HD, (head + 1) * HD)
        out_ref[head, :rows] = side_by_side(k[:, at], v[:, at])
        out_ref[head, rows:] = side_by_side(q[:, at], g[:, at])


def pack(query, keys, values, grad_out):
    rows, width = query.shape
    return pl.pallas_call(
        pack_kernel,
        out_shape=pltpu.VMEM((width // HD, 2 * rows, PAIR), query.dtype),
        in_specs=[VMEM] * 4,
        out_specs=VMEM,
        name="pack_heads",
    )(query, keys, values, grad_out)


def attend_kernel(shares, *refs):
    blocks = refs[:shares]
    valid_ref, views_ref, bias_ref, out_ref = refs[shares : shares + 4]
    base_ref, turn_ref, kv_ref, qg_ref, flip_ref, sum_ref, dq_ref = refs[shares + 4 :]
    homes, rows = blocks[0].shape[0], blocks[0].shape[1] // 2
    own = homes * rows
    tokens = own * shares
    per_home, per_tile = rows // FRAME, TILE // rows
    tiles, chunks, own_chunks = own // TILE, tokens // CHUNK, own // CHUNK
    mine = lax.axis_index("share")
    bias = bias_ref[lax.axis_index("heads")] * LOG2E
    slot = lax.broadcasted_iota(jnp.int32, (FRAME, TILE), 0)
    lane = lax.broadcasted_iota(jnp.int32, (1, TILE), 1)

    def frame_of(block, home, which):
        share = lax.rem(mine + block, shares)
        return (home * shares + share) * per_home + which

    for block in range(shares):
        start = block * own
        for home in range(homes):
            here = slice(start + home * rows, start + (home + 1) * rows)
            kv_ref[here, :] = blocks[block][home, :rows]
            qg_ref[here, :] = blocks[block][home, rows:]
            for which in range(per_home):
                frame = frame_of(block, home, which)
                exo = views_ref[frame] != 0
                live = slot < valid_ref[frame]
                here = slice(
                    start + home * rows + which * FRAME,
                    start + home * rows + (which + 1) * FRAME,
                )
                base_ref[here, :] = jnp.where(live, jnp.where(exo, bias, 0.0), DEAD)
                turn_ref[here, :] = jnp.where(live, jnp.where(exo, 0.0, bias), DEAD)
        here = slice(start, start + own)
        flip_ref[:, here] = kv_ref[here, :].astype(jnp.float32).T.astype(jnp.bfloat16)

    sum_ref[...] = jnp.zeros_like(sum_ref)
    low = lax.broadcasted_iota(jnp.int32, (TILE, PAIR), 1) < HD
    contract_last = (((1,), (1,)), ((), ()))

    def tile(ours, index):
        here = pl.ds(pl.multiple_of(index * TILE, TILE), TILE)
        qg = qg_ref[here, :].astype(jnp.float32)
        weights = jnp.concatenate(
            [jnp.where(low, qg, 0.0), jnp.where(low, 0.0, qg)], axis=0
        ).astype(jnp.bfloat16)
        block, first = lax.div(index, tiles), lax.rem(index, tiles) * per_tile
        label = jnp.zeros((1, TILE), jnp.int32)
        for part in range(TILE // FRAME):
            view = views_ref[frame_of(block, first + part // per_home, part % per_home)]
            label = jnp.where(lane // FRAME == part, view, label)
        exo = label != 0

        both = lax.dot_general(
            kv_ref[...], weights, contract_last, preferred_element_type=jnp.float32
        )
        tops, totals, mixes, expos = [], [], [], []
        for c in range(chunks):
            at = slice(c * CHUNK, (c + 1) * CHUNK)
            logits = both[at, :TILE] * (SCALE * LOG2E) + jnp.where(
                exo, turn_ref[at, :], base_ref[at, :]
            )
            top = jnp.max(logits, axis=0, keepdims=True)
            expo = jnp.exp2(logits - top)
            expos.append(expo)
            tops.append(top)
            totals.append(jnp.sum(expo, axis=0, keepdims=True))
            mixes.append(jnp.sum(expo * both[at, TILE:], axis=0, keepdims=True))
        highest = functools.reduce(jnp.maximum, tops)
        factors = [jnp.exp2(top - highest) for top in tops]
        inverse = 1.0 / sum(f * t for f, t in zip(factors, totals))
        delta = sum(f * m for f, m in zip(factors, mixes)) * inverse

        lows, grads = [], []
        for c in range(chunks if ours else own_chunks):
            at = slice(c * CHUNK, (c + 1) * CHUNK)
            weight = expos[c] * (factors[c] * inverse)
            grads.append(
                ((weight * SCALE) * (both[at, TILE:] - delta)).astype(jnp.bfloat16)
            )
            if c < own_chunks:
                lows.append(weight.astype(jnp.bfloat16))
        sum_ref[...] += jnp.dot(
            side_by_side(
                jnp.concatenate(grads[:own_chunks], axis=0), jnp.concatenate(lows, axis=0)
            ),
            weights,
            preferred_element_type=jnp.float32,
        )
        if ours:
            turned = jnp.dot(
                flip_ref[...],
                jnp.concatenate(grads, axis=0),
                preferred_element_type=jnp.float32,
            )
            dq_ref[here, :] = turned.T

    pl.loop(0, tiles, unroll=UNROLL)(functools.partial(tile, True))
    pl.loop(tiles, tiles * shares, unroll=UNROLL)(functools.partial(tile, False))
    out_ref[:, :rows, :] = sum_ref[...].astype(jnp.bfloat16).reshape(homes, rows, PAIR)
    for home in range(homes):
        start, half = home * rows, rows // 2
        out_ref[home, rows:, :] = side_by_side(
            dq_ref[start : start + half, :HD], dq_ref[start + half : start + rows, :HD]
        ).astype(jnp.bfloat16)


def attend(blocks, valid, views, cross_bias):
    homes, both, _ = blocks[0].shape
    rows = both // 2
    own = homes * rows
    tokens = own * len(blocks)
    return pl.pallas_call(
        functools.partial(attend_kernel, len(blocks)),
        out_shape=jax.ShapeDtypeStruct((homes, rows + rows // 2, PAIR), jnp.bfloat16),
        in_specs=[VMEM] * len(blocks) + [SMEM] * 3,
        out_specs=VMEM,
        scratch_shapes=[
            pltpu.VMEM((tokens, TILE), jnp.float32),
            pltpu.VMEM((tokens, TILE), jnp.float32),
            pltpu.VMEM((tokens, PAIR), jnp.bfloat16),
            pltpu.VMEM((tokens, PAIR), jnp.bfloat16),
            pltpu.VMEM((PAIR, tokens), jnp.bfloat16),
            pltpu.VMEM((own, PAIR), jnp.float32),
            pltpu.VMEM((own, PAIR), jnp.float32),
        ],
        compiler_params=pltpu.CompilerParams(vmem_limit_bytes=LIMIT),
        name="attend_backward",
    )(*blocks, valid, views, cross_bias)


def unpack_kernel(in_ref, dq_ref, dk_ref, dv_ref):
    rows = dq_ref.shape[0]
    half = rows // 2
    for head in range(0, in_ref.shape[0], 2):
        columns = slice(head * HD, (head + 2) * HD)
        one, two = (in_ref[head + which].astype(jnp.float32) for which in (0, 1))
        left = side_by_side(one[:, :HD], two[:, :HD])
        right = side_by_side(one[:, HD:], two[:, HD:])
        dk_ref[:, columns] = left[:rows]
        dv_ref[:, columns] = right[:rows]
        dq_ref[:half, columns] = left[rows:]
        dq_ref[half:, columns] = right[rows:]


def unpack(given, rows):
    shape = jax.ShapeDtypeStruct((rows, given.shape[0] * HD), jnp.float32)
    return pl.pallas_call(
        unpack_kernel,
        out_shape=(shape,) * 3,
        in_specs=[VMEM],
        out_specs=(VMEM,) * 3,
        name="unpack_heads",
    )(pltpu.with_memory_space_constraint(given, pltpu.VMEM))


def local(query, keys, values, grad_out, valid, views, cross_bias):
    swap = functools.partial(
        lax.all_to_all, axis_name="heads", split_axis=0, concat_axis=0, tiled=True
    )
    shares = lax.axis_size("share")
    mine = swap(pack(query, keys, values, grad_out))
    blocks = [mine] + [
        lax.ppermute(mine, "share", [((i + k) % shares, i) for i in range(shares)])
        for k in range(1, shares)
    ]
    return unpack(swap(attend(blocks, valid, views, cross_bias)), query.shape[0])


def solution(mesh):
    groups = mesh.shape["grp"]
    members = mesh.shape["blk"] * mesh.shape["head"]

    def run(query, keys, values, grad_out, valid, views, cross_bias):
        heads = query.shape[1] // HD
        layout = Mesh(
            mesh.devices.reshape(groups, heads, members // heads), ("grp", "heads", "share")
        )
        tokens = P(("grp", "heads", "share"), None)
        return jax.shard_map(
            local,
            mesh=layout,
            in_specs=(tokens,) * 4 + (P("grp"), P("grp"), P()),
            out_specs=(tokens,) * 3,
            check_vma=False,
        )(query, keys, values, grad_out, valid, views, cross_bias)

    return run
```

profile of v0, /device:TPU:0, one launch (start us, length us, event | category | flops | bytes accessed | tf_op | source)
XLA Modules:
  0.0 36.9 jit_solution(11166114395041188859)
XLA Ops:
  0.6 1.1 %pack_heads.1 = bf16[8,128,128]{2,1,0:T(8,128)(2,1)S(1)} custom-call(bf16[64,512]{1,0:T(8,128)(2,1)} %q_ref.1, bf16[64,512]{1,0:T(8,128)(2,1)} %k_ref.1, bf16[64,512]{1,0:T(8,128)(2,1)} %v_ref.1, bf16[64,512]{1,0:T(8,128)(2,1)} %g_ref.1), custom_call_target="tpu_custom_call" | custom-call | tf_op jit(solution)/shard_map/pack_heads/pallas_call | solution.py:42
  1.7 0.0 copy-start
  1.7 0.0 copy-start.1
  1.7 0.0 copy-start.2
  1.7 16.1 %all_to_all.10.refs_0_ = bf16[8,128,128]{2,1,0:T(8,128)(2,1)S(1)} all-to-all(bf16[8,128,128]{2,1,0:T(8,128)(2,1)S(1)} %pack_heads.1), channel_id=1, replica_groups=mesh['grp'=2,'blk'=4,'head'=4] {'blk','head':(1)2}, dimensions={0} | all-to-all | bytes 524288 | tf_op jit(solution)/shard_map/all_to_all | solution.py:213
  17.8 0.0 collective-permute-start
  17.8 1.5 %collective-permute-done.refs_1_ = bf16[8,128,128]{2,1,0:T(8,128)(2,1)S(1)} collective-permute-done((bf16[8,128,128]{2,1,0:T(8,128)(2,1)S(1)}, bf16[8,128,128]{2,1,0:T(8,128)(2,1)S(1)}, u32[]{:S(2)}, u32[]{:S(2)}) %collective-permute-start) | collective-permute-done | bytes 262176 | tf_op jit(solution)/shard_map/ppermute | solution.py:215
  19.4 0.0 copy-done
  19.4 0.0 copy-done.1
  19.4 0.0 copy-done.2
  19.4 5.0 %attend_backward.1 = bf16[8,96,128]{2,1,0:T(8,128)(2,1)S(1)} custom-call(bf16[8,128,128]{2,1,0:T(8,128)(2,1)S(1)} %all_to_all.10.refs_0_, bf16[8,128,128]{2,1,0:T(8,128)(2,1)S(1)} %collective-permute-done.refs_1_, s32[32]{0:T(128)S(1)} %copy-done, s32[32]{0:T(128)S(1)} %copy-done.1, f32[8]{0:T(128)S(1)} %copy-done.2), custom_call_target="tpu_custom_call" | custom-call | tf_op jit(solution)/shard_map/attend_backward/pallas_call | solution.py:164
  24.4 11.6 %all_to_all.11.in_ref = bf16[8,96,128]{2,1,0:T(8,128)(2,1)S(1)} all-to-all(bf16[8,96,128]{2,1,0:T(8,128)(2,1)S(1)} %attend_backward.1), channel_id=1, replica_groups=mesh['grp'=2,'blk'=4,'head'=4] {'blk','head':(1)2}, dimensions={0} | all-to-all | bytes 393216 | tf_op jit(solution)/shard_map/all_to_all | solution.py:218
  36.1 0.9 %unpack_heads.1 = (f32[64,512]{1,0:T(8,128)}, f32[64,512]{1,0:T(8,128)}, f32[64,512]{1,0:T(8,128)}) custom-call(bf16[8,96,128]{2,1,0:T(8,128)(2,1)S(1)} %all_to_all.11.in_ref), custom_call_target="tpu_custom_call" | custom-call | tf_op jit(solution)/shard_map/unpack_heads/pallas_call | solution.py:199
Async XLA Ops:
  1.7 17.7 %copy-start = (s32[32]{0:T(128)S(1)}, s32[32]{0:T(128)}, u32[]{:S(2)}) copy-start(s32[32]{0:T(128)} %refs_2_.1) | copy-start | bytes 388
  1.7 17.7 %copy-start.1 = (s32[32]{0:T(128)S(1)}, s32[32]{0:T(128)}, u32[]{:S(2)}) copy-start(s32[32]{0:T(128)} %refs_3_.1) | copy-start | bytes 388
  1.7 17.7 %copy-start.2 = (f32[8]{0:T(128)S(1)}, f32[8]{0:T(128)}, u32[]{:S(2)}) copy-start(f32[8]{0:T(128)} %refs_4_.1) | copy-start | bytes 100
  17.8 1.5 %collective-permute-start = (bf16[8,128,128]{2,1,0:T(8,128)(2,1)S(1)}, bf16[8,128,128]{2,1,0:T(8,128)(2,1)S(1)}, u32[]{:S(2)}, u32[]{:S(2)}) collective-permute-start(bf16[8,128,128]{2,1,0:T(8,128)(2,1)S(1)} %all_to_all.10.refs_0_), channel_id=1, source_target_pairs={{1,0},{0,1},{3,2},{2,3},{5,4},{4,5},{7,6},{6,7},{9,8},{8,9},{11,10... | collective-permute-start | bytes 786440 | tf_op jit(solution)/shard_map/ppermute | solution.py:215
where the time goes:
time: 37.2 us; the launch traced here: 36.9 us
  blocking collectives  27.7 us (74%)
  Pallas kernels  6.94 us (19%)
  waiting for transfers between devices  1.53 us (4%)
  between operations  0.68 us (2%)
    all_to_all x1, blocking collectives, local(): mine = swap(pack(query, keys, values, grad_out))  16.1 us
    all_to_all x1, blocking collectives, local(): swap(attend(blocks, valid, views, cross_bias))  11.6 us
    pallas_call x1, Pallas kernels, attend(): pl.pallas_call(functools.partial(attend_kernel, len(blocks)), out_shape=j...  5.02 us
    ppermute x1, waiting for transfers between devices, local(): lax.ppermute(mine, 'share', [((i + k) % shares, i) for i in range(shares)])  1.53 us
    pallas_call x1, Pallas kernels, pack(): pl.pallas_call(pack_kernel, out_shape=pltpu.VMEM((width // HD, 2 * rows,...  1.07 us
    pallas_call x1, Pallas kernels, unpack(): pl.pallas_call(unpack_kernel, out_shape=(shape,) * 3, in_specs=[VMEM], ou...  0.85 us
  transfers between devices with their start and end apart: 1, of which 1 were waited for; matrix products, arithmetic and copies ran while one was open for 0% of the time, Pallas kernels for 0%

commit v1 on v0

--- a/solution.py
+++ b/solution.py
@@ -13,7 +13,7 @@
 PAIR = 2 * HD
 TILE = 128
 CHUNK = 128
-UNROLL = 2
+UNROLL = 4
 
 SCALE = 0.125
 DEAD = -1e30

time: 37.2 us -> 35.7 us (0.960)
  Pallas kernels: 6.94 us -> 5.52 us
    pallas_call x1, Pallas kernels: 5.02 us -> 3.6 us  [attend(): pl.pallas_call(functools.partial(attend_kernel, len(blocks)), out_shape=j...]
where the time goes in v1:
time: 35.7 us; the launch traced here: 35.5 us
  blocking collectives  27.7 us (78%)
  Pallas kernels  5.52 us (15%)
  waiting for transfers between devices  1.53 us (4%)
  between operations  0.68 us (2%)
    all_to_all x1, blocking collectives, local(): mine = swap(pack(query, keys, values, grad_out))  16.1 us
    all_to_all x1, blocking collectives, local(): swap(attend(blocks, valid, views, cross_bias))  11.6 us
    pallas_call x1, Pallas kernels, attend(): pl.pallas_call(functools.partial(attend_kernel, len(blocks)), out_shape=j...  3.6 us
    ppermute x1, waiting for transfers between devices, local(): lax.ppermute(mine, 'share', [((i + k) % shares, i) for i in range(shares)])  1.53 us
    pallas_call x1, Pallas kernels, pack(): pl.pallas_call(pack_kernel, out_shape=pltpu.VMEM((width // HD, 2 * rows,...  1.07 us
    pallas_call x1, Pallas kernels, unpack(): pl.pallas_call(unpack_kernel, out_shape=(shape,) * 3, in_specs=[VMEM], ou...  0.85 us
  transfers between devices with their start and end apart: 1, of which 1 were waited for; matrix products, arithmetic and copies ran while one was open for 0% of the time, Pallas kernels for 0%

profile of v1, /device:TPU:0, one launch (start us, length us, event | category | flops | bytes accessed | tf_op | source)
XLA Modules:
  0.0 35.5 jit_solution(3784659201338759872)
XLA Ops:
  0.6 1.1 %pack_heads.1 = bf16[8,128,128]{2,1,0:T(8,128)(2,1)S(1)} custom-call(bf16[64,512]{1,0:T(8,128)(2,1)} %q_ref.1, bf16[64,512]{1,0:T(8,128)(2,1)} %k_ref.1, bf16[64,512]{1,0:T(8,128)(2,1)} %v_ref.1, bf16[64,512]{1,0:T(8,128)(2,1)} %g_ref.1), custom_call_target="tpu_custom_call" | custom-call | tf_op jit(solution)/shard_map/pack_heads/pallas_call | solution.py:42
  1.7 0.0 copy-start
  1.7 0.0 copy-start.1
  1.7 0.0 copy-start.2
  1.7 16.1 %all_to_all.10.refs_0_ = bf16[8,128,128]{2,1,0:T(8,128)(2,1)S(1)} all-to-all(bf16[8,128,128]{2,1,0:T(8,128)(2,1)S(1)} %pack_heads.1), channel_id=1, replica_groups=mesh['grp'=2,'blk'=4,'head'=4] {'blk','head':(1)2}, dimensions={0} | all-to-all | bytes 524288 | tf_op jit(solution)/shard_map/all_to_all | solution.py:213
  17.8 0.0 collective-permute-start
  17.8 1.5 %collective-permute-done.refs_1_ = bf16[8,128,128]{2,1,0:T(8,128)(2,1)S(1)} collective-permute-done((bf16[8,128,128]{2,1,0:T(8,128)(2,1)S(1)}, bf16[8,128,128]{2,1,0:T(8,128)(2,1)S(1)}, u32[]{:S(2)}, u32[]{:S(2)}) %collective-permute-start) | collective-permute-done | bytes 262176 | tf_op jit(solution)/shard_map/ppermute | solution.py:215
  19.4 0.0 copy-done
  19.4 0.0 copy-done.1
  19.4 0.0 copy-done.2
  19.4 3.6 %attend_backward.1 = bf16[8,96,128]{2,1,0:T(8,128)(2,1)S(1)} custom-call(bf16[8,128,128]{2,1,0:T(8,128)(2,1)S(1)} %all_to_all.10.refs_0_, bf16[8,128,128]{2,1,0:T(8,128)(2,1)S(1)} %collective-permute-done.refs_1_, s32[32]{0:T(128)S(1)} %copy-done, s32[32]{0:T(128)S(1)} %copy-done.1, f32[8]{0:T(128)S(1)} %copy-done.2), custom_call_target="tpu_custom_call" | custom-call | tf_op jit(solution)/shard_map/attend_backward/pallas_call | solution.py:164
  23.0 11.6 %all_to_all.11.in_ref = bf16[8,96,128]{2,1,0:T(8,128)(2,1)S(1)} all-to-all(bf16[8,96,128]{2,1,0:T(8,128)(2,1)S(1)} %attend_backward.1), channel_id=1, replica_groups=mesh['grp'=2,'blk'=4,'head'=4] {'blk','head':(1)2}, dimensions={0} | all-to-all | bytes 393216 | tf_op jit(solution)/shard_map/all_to_all | solution.py:218
  34.6 0.9 %unpack_heads.1 = (f32[64,512]{1,0:T(8,128)}, f32[64,512]{1,0:T(8,128)}, f32[64,512]{1,0:T(8,128)}) custom-call(bf16[8,96,128]{2,1,0:T(8,128)(2,1)S(1)} %all_to_all.11.in_ref), custom_call_target="tpu_custom_call" | custom-call | tf_op jit(solution)/shard_map/unpack_heads/pallas_call | solution.py:199
Async XLA Ops:
  1.7 17.7 %copy-start = (s32[32]{0:T(128)S(1)}, s32[32]{0:T(128)}, u32[]{:S(2)}) copy-start(s32[32]{0:T(128)} %refs_2_.1) | copy-start | bytes 388
  1.7 17.7 %copy-start.1 = (s32[32]{0:T(128)S(1)}, s32[32]{0:T(128)}, u32[]{:S(2)}) copy-start(s32[32]{0:T(128)} %refs_3_.1) | copy-start | bytes 388
  1.7 17.7 %copy-start.2 = (f32[8]{0:T(128)S(1)}, f32[8]{0:T(128)}, u32[]{:S(2)}) copy-start(f32[8]{0:T(128)} %refs_4_.1) | copy-start | bytes 100
  17.8 1.5 %collective-permute-start = (bf16[8,128,128]{2,1,0:T(8,128)(2,1)S(1)}, bf16[8,128,128]{2,1,0:T(8,128)(2,1)S(1)}, u32[]{:S(2)}, u32[]{:S(2)}) collective-permute-start(bf16[8,128,128]{2,1,0:T(8,128)(2,1)S(1)} %all_to_all.10.refs_0_), channel_id=1, source_target_pairs={{1,0},{0,1},{3,2},{2,3},{5,4},{4,5},{7,6},{6,7},{9,8},{8,9},{11,10... | collective-permute-start | bytes 786440 | tf_op jit(solution)/shard_map/ppermute | solution.py:215

commit v2 on v1

--- a/solution.py
+++ b/solution.py
@@ -51,16 +51,25 @@
 def attend_kernel(shares, *refs):
     blocks = refs[:shares]
     valid_ref, views_ref, bias_ref, out_ref = refs[shares : shares + 4]
-    base_ref, turn_ref, kv_ref, qg_ref, flip_ref, sum_ref, dq_ref = refs[shares + 4 :]
+    kv_ref, qg_ref, flip_ref, sum_ref, dq_ref = refs[shares + 4 :]
     homes, rows = blocks[0].shape[0], blocks[0].shape[1] // 2
     own = homes * rows
     tokens = own * shares
     per_home, per_tile = rows // FRAME, TILE // rows
     tiles, chunks, own_chunks = own // TILE, tokens // CHUNK, own // CHUNK
     mine = lax.axis_index("share")
-    bias = bias_ref[lax.axis_index("heads")] * LOG2E
-    slot = lax.broadcasted_iota(jnp.int32, (FRAME, TILE), 0)
-    lane = lax.broadcasted_iota(jnp.int32, (1, TILE), 1)
+    unroll = UNROLL if shares <= 2 else 1
+    slot = lax.broadcasted_iota(jnp.int32, (FRAME, PAIR), 0)
+    lane = lax.broadcasted_iota(jnp.int32, (1, PAIR), 1)
+
+    bias = jnp.full((1, PAIR), bias_ref[lax.axis_index("heads")] / SCALE, jnp.float32)
+    high = bias.astype(jnp.bfloat16).astype(jnp.float32)
+    middle = (bias - high).astype(jnp.bfloat16).astype(jnp.float32)
+    part = lax.rem(lane, 3)
+    parts = jnp.where(part == 0, high, jnp.where(part == 1, middle, bias - high - middle))
+    dead = jnp.where(lane == 6, DEAD / SCALE, 0.0)
+    of_exo_query = jnp.where(lane < 3, parts, dead)
+    of_ego_query = jnp.where((lane >= 3) & (lane < 6), parts, dead)
 
     def frame_of(block, home, which):
         share = lax.rem(mine + block, shares)
@@ -70,20 +79,20 @@
         start = block * own
         for home in range(homes):
             here = slice(start + home * rows, start + (home + 1) * rows)
-            kv_ref[here, :] = blocks[block][home, :rows]
+            kv_ref[here, :PAIR] = blocks[block][home, :rows]
             qg_ref[here, :] = blocks[block][home, rows:]
             for which in range(per_home):
                 frame = frame_of(block, home, which)
-                exo = views_ref[frame] != 0
-                live = slot < valid_ref[frame]
+                first = jnp.where(views_ref[frame] != 0, 3, 0)
+                marks = jnp.where((lane >= first) & (lane < first + 3), 1.0, 0.0)
+                gone = jnp.where(slot < valid_ref[frame], 0.0, 1.0)
                 here = slice(
                     start + home * rows + which * FRAME,
                     start + home * rows + (which + 1) * FRAME,
                 )
-                base_ref[here, :] = jnp.where(live, jnp.where(exo, bias, 0.0), DEAD)
-                turn_ref[here, :] = jnp.where(live, jnp.where(exo, 0.0, bias), DEAD)
+                kv_ref[here, PAIR:] = jnp.where(lane == 6, gone, marks).astype(jnp.bfloat16)
         here = slice(start, start + own)
-        flip_ref[:, here] = kv_ref[here, :].astype(jnp.float32).T.astype(jnp.bfloat16)
+        flip_ref[:, here] = kv_ref[here, :PAIR].astype(jnp.float32).T.astype(jnp.bfloat16)
 
     sum_ref[...] = jnp.zeros_like(sum_ref)
     low = lax.broadcasted_iota(jnp.int32, (TILE, PAIR), 1) < HD
@@ -96,29 +105,31 @@
             [jnp.where(low, qg, 0.0), jnp.where(low, 0.0, qg)], axis=0
         ).astype(jnp.bfloat16)
         block, first = lax.div(index, tiles), lax.rem(index, tiles) * per_tile
-        label = jnp.zeros((1, TILE), jnp.int32)
+        marks = []
         for part in range(TILE // FRAME):
             view = views_ref[frame_of(block, first + part // per_home, part % per_home)]
-            label = jnp.where(lane // FRAME == part, view, label)
-        exo = label != 0
+            row = jnp.where(view != 0, of_exo_query, of_ego_query)
+            marks.append(jnp.broadcast_to(row, (FRAME, PAIR)))
+        marks.append(jnp.zeros((TILE, PAIR), jnp.float32))
+        marks = jnp.concatenate(marks, axis=0).astype(jnp.bfloat16)
 
         both = lax.dot_general(
-            kv_ref[...], weights, contract_last, preferred_element_type=jnp.float32
+            kv_ref[...],
+            side_by_side(weights, marks),
+            contract_last,
+            preferred_element_type=jnp.float32,
         )
         tops, totals, mixes, expos = [], [], [], []
         for c in range(chunks):
             at = slice(c * CHUNK, (c + 1) * CHUNK)
-            logits = both[at, :TILE] * (SCALE * LOG2E) + jnp.where(
-                exo, turn_ref[at, :], base_ref[at, :]
-            )
-            top = jnp.max(logits, axis=0, keepdims=True)
-            expo = jnp.exp2(logits - top)
+            top = jnp.max(both[at, :TILE], axis=0, keepdims=True)
+            expo = jnp.exp2((both[at, :TILE] - top) * (SCALE * LOG2E))
             expos.append(expo)
             tops.append(top)
             totals.append(jnp.sum(expo, axis=0, keepdims=True))
             mixes.append(jnp.sum(expo * both[at, TILE:], axis=0, keepdims=True))
         highest = functools.reduce(jnp.maximum, tops)
-        factors = [jnp.exp2(top - highest) for top in tops]
+        factors = [jnp.exp2((top - highest) * (SCALE * LOG2E)) for top in tops]
         inverse = 1.0 / sum(f * t for f, t in zip(factors, totals))
         delta = sum(f * m for f, m in zip(factors, mixes)) * inverse
 
@@ -146,8 +157,8 @@
             )
             dq_ref[here, :] = turned.T
 
-    pl.loop(0, tiles, unroll=UNROLL)(functools.partial(tile, True))
-    pl.loop(tiles, tiles * shares, unroll=UNROLL)(functools.partial(tile, False))
+    pl.loop(0, tiles, unroll=unroll)(functools.partial(tile, True))
+    pl.loop(tiles, tiles * shares, unroll=unroll)(functools.partial(tile, False))
     out_ref[:, :rows, :] = sum_ref[...].astype(jnp.bfloat16).reshape(homes, rows, PAIR)
     for home in range(homes):
         start, half = home * rows, rows // 2
@@ -167,9 +178,7 @@
         in_specs=[VMEM] * len(blocks) + [SMEM] * 3,
         out_specs=VMEM,
         scratch_shapes=[
-            pltpu.VMEM((tokens, TILE), jnp.float32),
-            pltpu.VMEM((tokens, TILE), jnp.float32),
-            pltpu.VMEM((tokens, PAIR), jnp.bfloat16),
+            pltpu.VMEM((tokens, 2 * PAIR), jnp.bfloat16),
             pltpu.VMEM((tokens, PAIR), jnp.bfloat16),
             pltpu.VMEM((PAIR, tokens), jnp.bfloat16),
             pltpu.VMEM((own, PAIR), jnp.float32),

time: 35.7 us -> 35.6 us (level)
  no operation moved by 1% of the time
where the time goes in v2:
time: 35.6 us; the launch traced here: 35.4 us
  blocking collectives  27.7 us (78%)
  Pallas kernels  5.39 us (15%)
  waiting for transfers between devices  1.53 us (4%)
  between operations  0.68 us (2%)
    all_to_all x1, blocking collectives, local(): mine = swap(pack(query, keys, values, grad_out))  16.1 us
    all_to_all x1, blocking collectives, local(): swap(attend(blocks, valid, views, cross_bias))  11.6 us
    pallas_call x1, Pallas kernels, attend(): pl.pallas_call(functools.partial(attend_kernel, len(blocks)), out_shape=j...  3.46 us
    ppermute x1, waiting for transfers between devices, local(): lax.ppermute(mine, 'share', [((i + k) % shares, i) for i in range(shares)])  1.53 us
    pallas_call x1, Pallas kernels, pack(): pl.pallas_call(pack_kernel, out_shape=pltpu.VMEM((width // HD, 2 * rows,...  1.07 us
    pallas_call x1, Pallas kernels, unpack(): pl.pallas_call(unpack_kernel, out_shape=(shape,) * 3, in_specs=[VMEM], ou...  0.85 us
  transfers between devices with their start and end apart: 1, of which 1 were waited for; matrix products, arithmetic and copies ran while one was open for 0% of the time, Pallas kernels for 0%

profile of v2, /device:TPU:0, one launch (start us, length us, event | category | flops | bytes accessed | tf_op | source)
XLA Modules:
  0.0 35.4 jit_solution(7089418382517438457)
XLA Ops:
  0.6 1.1 %pack_heads.1 = bf16[8,128,128]{2,1,0:T(8,128)(2,1)S(1)} custom-call(bf16[64,512]{1,0:T(8,128)(2,1)} %q_ref.1, bf16[64,512]{1,0:T(8,128)(2,1)} %k_ref.1, bf16[64,512]{1,0:T(8,128)(2,1)} %v_ref.1, bf16[64,512]{1,0:T(8,128)(2,1)} %g_ref.1), custom_call_target="tpu_custom_call" | custom-call | tf_op jit(solution)/shard_map/pack_heads/pallas_call | solution.py:42
  1.7 0.0 copy-start
  1.7 0.0 copy-start.1
  1.7 0.0 copy-start.2
  1.7 16.1 %all_to_all.10.refs_0_ = bf16[8,128,128]{2,1,0:T(8,128)(2,1)S(1)} all-to-all(bf16[8,128,128]{2,1,0:T(8,128)(2,1)S(1)} %pack_heads.1), channel_id=1, replica_groups=mesh['grp'=2,'blk'=4,'head'=4] {'blk','head':(1)2}, dimensions={0} | all-to-all | bytes 524288 | tf_op jit(solution)/shard_map/all_to_all | solution.py:222
  17.8 0.0 collective-permute-start
  17.8 1.5 %collective-permute-done.refs_1_ = bf16[8,128,128]{2,1,0:T(8,128)(2,1)S(1)} collective-permute-done((bf16[8,128,128]{2,1,0:T(8,128)(2,1)S(1)}, bf16[8,128,128]{2,1,0:T(8,128)(2,1)S(1)}, u32[]{:S(2)}, u32[]{:S(2)}) %collective-permute-start) | collective-permute-done | bytes 262176 | tf_op jit(solution)/shard_map/ppermute | solution.py:224
  19.4 0.0 copy-done
  19.4 0.0 copy-done.1
  19.4 0.0 copy-done.2
  19.4 3.5 %attend_backward.1 = bf16[8,96,128]{2,1,0:T(8,128)(2,1)S(1)} custom-call(bf16[8,128,128]{2,1,0:T(8,128)(2,1)S(1)} %all_to_all.10.refs_0_, bf16[8,128,128]{2,1,0:T(8,128)(2,1)S(1)} %collective-permute-done.refs_1_, s32[32]{0:T(128)S(1)} %copy-done, s32[32]{0:T(128)S(1)} %copy-done.1, f32[8]{0:T(128)S(1)} %copy-done.2), custom_call_target="tpu_custom_call" | custom-call | tf_op jit(solution)/shard_map/attend_backward/pallas_call | solution.py:175
  22.9 11.6 %all_to_all.11.in_ref = bf16[8,96,128]{2,1,0:T(8,128)(2,1)S(1)} all-to-all(bf16[8,96,128]{2,1,0:T(8,128)(2,1)S(1)} %attend_backward.1), channel_id=1, replica_groups=mesh['grp'=2,'blk'=4,'head'=4] {'blk','head':(1)2}, dimensions={0} | all-to-all | bytes 393216 | tf_op jit(solution)/shard_map/all_to_all | solution.py:227
  34.5 0.9 %unpack_heads.1 = (f32[64,512]{1,0:T(8,128)}, f32[64,512]{1,0:T(8,128)}, f32[64,512]{1,0:T(8,128)}) custom-call(bf16[8,96,128]{2,1,0:T(8,128)(2,1)S(1)} %all_to_all.11.in_ref), custom_call_target="tpu_custom_call" | custom-call | tf_op jit(solution)/shard_map/unpack_heads/pallas_call | solution.py:208
Async XLA Ops:
  1.7 17.7 %copy-start = (s32[32]{0:T(128)S(1)}, s32[32]{0:T(128)}, u32[]{:S(2)}) copy-start(s32[32]{0:T(128)} %refs_2_.1) | copy-start | bytes 388
  1.7 17.7 %copy-start.1 = (s32[32]{0:T(128)S(1)}, s32[32]{0:T(128)}, u32[]{:S(2)}) copy-start(s32[32]{0:T(128)} %refs_3_.1) | copy-start | bytes 388
  1.7 17.7 %copy-start.2 = (f32[8]{0:T(128)S(1)}, f32[8]{0:T(128)}, u32[]{:S(2)}) copy-start(f32[8]{0:T(128)} %refs_4_.1) | copy-start | bytes 100
  17.8 1.5 %collective-permute-start = (bf16[8,128,128]{2,1,0:T(8,128)(2,1)S(1)}, bf16[8,128,128]{2,1,0:T(8,128)(2,1)S(1)}, u32[]{:S(2)}, u32[]{:S(2)}) collective-permute-start(bf16[8,128,128]{2,1,0:T(8,128)(2,1)S(1)} %all_to_all.10.refs_0_), channel_id=1, source_target_pairs={{1,0},{0,1},{3,2},{2,3},{5,4},{4,5},{7,6},{6,7},{9,8},{8,9},{11,10... | collective-permute-start | bytes 786440 | tf_op jit(solution)/shard_map/ppermute | solution.py:224

commit v3 on v2

v3 whole, which is shorter than its diff:
```python
import functools
import math

import jax
import jax.numpy as jnp
from jax import lax
from jax.experimental import pallas as pl
from jax.experimental.pallas import tpu as pltpu
from jax.sharding import Mesh, PartitionSpec as P

HD = 64
FRAME = 32
PAIR = 2 * HD
TILE = 128
CHUNK = 128
UNROLL = 4

SCALE = 0.125
DEAD = -1e30
LOG2E = math.log2(math.e)
LIMIT = 48 * 1024 * 1024

VMEM = pl.BlockSpec(memory_space=pltpu.VMEM)
SMEM = pl.BlockSpec(memory_space=pltpu.SMEM)


def side_by_side(left, right):
    return jnp.concatenate([left, right], axis=1)


def pack_kernel(q_ref, k_ref, v_ref, g_ref, out_ref):
    rows, width = q_ref.shape
    q, k, v, g = q_ref[...], k_ref[...], v_ref[...], g_ref[...]
    for head in range(width // HD):
        at = slice(head * HD, (head + 1) * HD)
        out_ref[head, :rows] = side_by_side(k[:, at], v[:, at])
        out_ref[head, rows:] = side_by_side(q[:, at], g[:, at])


def pack(query, keys, values, grad_out):
    rows, width = query.shape
    return pl.pallas_call(
        pack_kernel,
        out_shape=pltpu.VMEM((width // HD, 2 * rows, PAIR), query.dtype),
        in_specs=[VMEM] * 4,
        out_specs=VMEM,
        name="pack_heads",
    )(query, keys, values, grad_out)


def frame_of(homes, shares, per_home, block, home, which):
    share = lax.rem(lax.axis_index("share") + block, shares)
    return (home * shares + share) * per_home + which


def query_weights(qg):
    qg = qg.astype(jnp.float32)
    low = lax.broadcasted_iota(jnp.int32, qg.shape, 1) < HD
    return jnp.concatenate(
        [jnp.where(low, qg, 0.0), jnp.where(low, 0.0, qg)], axis=0
    ).astype(jnp.bfloat16)


def products(keys, weights):
    return lax.dot_general(
        keys, weights, (((1,), (1,)), ((), ())), preferred_element_type=jnp.float32
    )


def exponentials(raw, gw):
    top = jnp.max(raw, axis=0, keepdims=True)
    expo = jnp.exp2((raw - top) * (SCALE * LOG2E))
    total = jnp.sum(expo, axis=0, keepdims=True)
    return expo, (top, total, jnp.sum(expo * gw, axis=0, keepdims=True))


def chunk_of(c):
    return slice(c * CHUNK, (c + 1) * CHUNK)


def begin_kernel(shares, mine_ref, valid_ref, views_ref, bias_ref, key_mark_ref,
                 query_mark_ref, weights_ref, flip_ref, expo_ref, gw_ref, stat_ref, keys_ref):
    homes, rows = mine_ref.shape[0], mine_ref.shape[1] // 2
    own = homes * rows
    per_home, per_tile, tiles = rows // FRAME, TILE // rows, own // TILE
    unroll = UNROLL if shares <= 2 else 1
    slot = lax.broadcasted_iota(jnp.int32, (FRAME, PAIR), 0)
    lane = lax.broadcasted_iota(jnp.int32, (1, PAIR), 1)

    bias = jnp.full((1, PAIR), bias_ref[lax.axis_index("heads")] / SCALE, jnp.float32)
    high = bias.astype(jnp.bfloat16).astype(jnp.float32)
    middle = (bias - high).astype(jnp.bfloat16).astype(jnp.float32)
    part = lax.rem(lane, 3)
    parts = jnp.where(part == 0, high, jnp.where(part == 1, middle, bias - high - middle))
    dead = jnp.where(lane == 6, DEAD / SCALE, 0.0)
    of_exo_query = jnp.where(lane < 3, parts, dead)
    of_ego_query = jnp.where((lane >= 3) & (lane < 6), parts, dead)

    for block in range(shares):
        for home in range(homes):
            for which in range(per_home):
                frame = frame_of(homes, shares, per_home, block, home, which)
                start = block * own + home * rows + which * FRAME
                here = slice(start, start + FRAME)
                exo = views_ref[frame] != 0
                first = jnp.where(exo, 3, 0)
                marks = jnp.where((lane >= first) & (lane < first + 3), 1.0, 0.0)
                gone = jnp.where(slot < valid_ref[frame], 0.0, 1.0)
                key_mark_ref[here, :] = jnp.where(lane == 6, gone, marks).astype(jnp.bfloat16)
                query_mark_ref[here, :] = jnp.broadcast_to(
                    jnp.where(exo, of_exo_query, of_ego_query), (FRAME, PAIR)
                ).astype(jnp.bfloat16)

    kv = mine_ref[:, :rows, :].reshape(own, PAIR)
    flip_ref[...] = kv.astype(jnp.float32).T.astype(jnp.bfloat16)
    keys_ref[:, :PAIR] = kv
    keys_ref[:, PAIR:] = key_mark_ref[:own, :]

    def tile(index):
        qg = mine_ref[pl.ds(index * per_tile, per_tile), rows:, :].reshape(TILE, PAIR)
        here = pl.ds(pl.multiple_of(index * TILE, TILE), TILE)
        marks = query_mark_ref[here, :]
        weights = side_by_side(
            query_weights(qg), jnp.concatenate([marks, jnp.zeros_like(marks)], axis=0)
        )
        weights_ref[index] = weights
        both = products(keys_ref[...], weights)
        gw_ref[index] = both[:, TILE:]
        for c in range(own // CHUNK):
            at = chunk_of(c)
            expo, stats = exponentials(both[at, :TILE], both[at, TILE:])
            expo_ref[index, at, :] = expo
            for which, stat in enumerate(stats):
                stat_ref[index, which, c : c + 1, :] = stat

    pl.loop(0, tiles, unroll=unroll)(tile)


def finish_kernel(shares, *refs):
    blocks, refs = refs[:shares], refs[shares:]
    key_mark_ref, query_mark_ref, weights_ref, own_flip_ref = refs[:4]
    expo_ref, gw_ref, stat_ref, out_ref, keys_ref, qg_ref, flip_ref, sum_ref, dq_ref = refs[4:]
    homes, rows = blocks[0].shape[0], blocks[0].shape[1] // 2
    own = homes * rows
    tokens = own * shares
    tiles, chunks, own_chunks = own // TILE, tokens // CHUNK, own // CHUNK
    unroll = UNROLL if shares <= 2 else 1

    keys_ref[:, PAIR:] = key_mark_ref[...]
    for block in range(shares):
        here = slice(block * own, (block + 1) * own)
        kv = blocks[block][:, :rows, :].reshape(own, PAIR)
        keys_ref[here, :PAIR] = kv
        if block:
            there = slice((block - 1) * own, block * own)
            flip_ref[:, there] = kv.astype(jnp.float32).T.astype(jnp.bfloat16)
            qg_ref[there, :] = blocks[block][:, rows:, :].reshape(own, PAIR)
    sum_ref[...] = jnp.zeros_like(sum_ref)

    def tile(ours, index):
        here = pl.ds(pl.multiple_of(index * TILE, TILE), TILE)
        if ours:
            weights = weights_ref[index]
            given = own_chunks
            if chunks > own_chunks:
                both = products(keys_ref[own:, :], weights)
        else:
            marks = query_mark_ref[pl.ds(pl.multiple_of(own + index * TILE, TILE), TILE), :]
            weights = side_by_side(
                query_weights(qg_ref[here, :]),
                jnp.concatenate([marks, jnp.zeros_like(marks)], axis=0),
            )
            given = 0
            both = products(keys_ref[...], weights)
        expos, gws, stats = [], [], []
        for c in range(chunks):
            if c < given:
                expos.append(expo_ref[index, chunk_of(c), :])
                gws.append(gw_ref[index, chunk_of(c), :])
                stats.append([stat_ref[index, which, c : c + 1, :] for which in range(3)])
            else:
                at = chunk_of(c - given)
                gws.append(both[at, TILE:])
                expo, stat = exponentials(both[at, :TILE], gws[-1])
                expos.append(expo)
                stats.append(stat)
        highest = functools.reduce(jnp.maximum, [top for top, _, _ in stats])
        factors = [jnp.exp2((top - highest) * (SCALE * LOG2E)) for top, _, _ in stats]
        inverse = 1.0 / sum(f * total for f, (_, total, _) in zip(factors, stats))
        delta = sum(f * mix for f, (_, _, mix) in zip(factors, stats)) * inverse

        lows, grads = [], []
        for c in range(chunks if ours else own_chunks):
            weight = expos[c] * (factors[c] * inverse)
            grads.append(((weight * SCALE) * (gws[c] - delta)).astype(jnp.bfloat16))
            if c < own_chunks:
                lows.append(weight.astype(jnp.bfloat16))
        own_grads = jnp.concatenate(grads[:own_chunks], axis=0)
        sum_ref[...] += jnp.dot(
            side_by_side(own_grads, jnp.concatenate(lows, axis=0)),
            weights[:, :PAIR],
            preferred_element_type=jnp.float32,
        )
        if ours:
            turned = jnp.dot(own_flip_ref[...], own_grads, preferred_element_type=jnp.float32)
            if chunks > own_chunks:
                turned += jnp.dot(
                    flip_ref[...],
                    jnp.concatenate(grads[own_chunks:], axis=0),
                    preferred_element_type=jnp.float32,
                )
            dq_ref[here, :] = turned.T

    pl.loop(0, tiles, unroll=unroll)(functools.partial(tile, True))
    pl.loop(0, tiles * (shares - 1), unroll=unroll)(functools.partial(tile, False))
    out_ref[:, :rows, :] = sum_ref[...].astype(jnp.bfloat16).reshape(homes, rows, PAIR)
    for home in range(homes):
        start, half = home * rows, rows // 2
        out_ref[home, rows:, :] = side_by_side(
            dq_ref[start : start + half, :HD], dq_ref[start + half : start + rows, :HD]
        ).astype(jnp.bfloat16)


def attend(mine, others, valid, views, cross_bias):
    shares = len(others) + 1
    homes, both, _ = mine.shape
    rows = both // 2
    own = homes * rows
    tokens, tiles = own * shares, own // TILE
    begun = pl.pallas_call(
        functools.partial(begin_kernel, shares),
        out_shape=(
            pltpu.VMEM((tokens, PAIR), jnp.bfloat16),
            pltpu.VMEM((tokens, PAIR), jnp.bfloat16),
            pltpu.VMEM((tiles, 2 * TILE, 2 * PAIR), jnp.bfloat16),
            pltpu.VMEM((PAIR, own), jnp.bfloat16),
            pltpu.VMEM((tiles, own, TILE), jnp.float32),
            pltpu.VMEM((tiles, own, TILE), jnp.float32),
            pltpu.VMEM((tiles, 3, own // CHUNK, TILE), jnp.float32),
        ),
        in_specs=[VMEM] + [SMEM] * 3,
        out_specs=(VMEM,) * 7,
        scratch_shapes=[pltpu.VMEM((own, 2 * PAIR), jnp.bfloat16)],
        compiler_params=pltpu.CompilerParams(vmem_limit_bytes=LIMIT),
        cost_estimate=pl.CostEstimate(
            flops=8 * own * own * PAIR, bytes_accessed=8 * own * own, transcendentals=own * own
        ),
        name="attend_begin",
    )(mine, valid, views, cross_bias)
    return pl.pallas_call(
        functools.partial(finish_kernel, shares),
        out_shape=pltpu.VMEM((homes, rows + rows // 2, PAIR), jnp.bfloat16),
        in_specs=[VMEM] * (shares + 7),
        out_specs=VMEM,
        scratch_shapes=[
            pltpu.VMEM((tokens, 2 * PAIR), jnp.bfloat16),
            pltpu.VMEM((max(tokens - own, TILE), PAIR), jnp.bfloat16),
            pltpu.VMEM((PAIR, max(tokens - own, TILE)), jnp.bfloat16),
            pltpu.VMEM((own, PAIR), jnp.float32),
            pltpu.VMEM((own, PAIR), jnp.float32),
        ],
        compiler_params=pltpu.CompilerParams(vmem_limit_bytes=LIMIT),
        name="attend_finish",
    )(mine, *others, *begun)


def unpack_kernel(in_ref, dq_ref, dk_ref, dv_ref):
    rows = dq_ref.shape[0]
    half = rows // 2
    for head in range(0, in_ref.shape[0], 2):
        columns = slice(head * HD, (head + 2) * HD)
        one, two = (in_ref[head + which].astype(jnp.float32) for which in (0, 1))
        left = side_by_side(one[:, :HD], two[:, :HD])
        right = side_by_side(one[:, HD:], two[:, HD:])
        dk_ref[:, columns] = left[:rows]
        dv_ref[:, columns] = right[:rows]
        dq_ref[:half, columns] = left[rows:]
        dq_ref[half:, columns] = right[rows:]


def unpack(given, rows):
    shape = jax.ShapeDtypeStruct((rows, given.shape[0] * HD), jnp.float32)
    return pl.pallas_call(
        unpack_kernel,
        out_shape=(shape,) * 3,
        in_specs=[VMEM],
        out_specs=(VMEM,) * 3,
        name="unpack_heads",
    )(pltpu.with_memory_space_constraint(given, pltpu.VMEM))


def local(query, keys, values, grad_out, valid, views, cross_bias):
    swap = functools.partial(
        lax.all_to_all, axis_name="heads", split_axis=0, concat_axis=0, tiled=True
    )
    shares = lax.axis_size("share")
    mine = swap(pack(query, keys, values, grad_out))
    others = [
        lax.ppermute(mine, "share", [((i + k) % shares, i) for i in range(shares)])
        for k in range(1, shares)
    ]
    given = attend(mine, others, valid, views, cross_bias)
    return unpack(swap(given), query.shape[0])


def solution(mesh):
    groups = mesh.shape["grp"]
    members = mesh.shape["blk"] * mesh.shape["head"]

    def run(query, keys, values, grad_out, valid, views, cross_bias):
        heads = query.shape[1] // HD
        layout = Mesh(
            mesh.devices.reshape(groups, heads, members // heads), ("grp", "heads", "share")
        )
        tokens = P(("grp", "heads", "share"), None)
        return jax.shard_map(
            local,
            mesh=layout,
            in_specs=(tokens,) * 4 + (P("grp"), P("grp"), P()),
            out_specs=(tokens,) * 3,
            check_vma=False,
        )(query, keys, values, grad_out, valid, views, cross_bias)

    return run
```

time: 35.6 us -> 36 us (1.011)
  Pallas kernels: 5.39 us -> 6.95 us
  waiting for transfers between devices: 1.53 us -> 0.27 us
    pallas_call x1 -> x2, Pallas kernels: 3.46 us -> 5.03 us  [the longest x1 3.79 us: attend(): pl.pallas_call(functools.partial(finish_kernel, shares), out_shape=pltpu....]
    ppermute x1, waiting for transfers between devices: 1.53 us -> 0.27 us  [local(): lax.ppermute(mine, 'share', [((i + k) % shares, i) for i in range(shares)])]
  transfers between devices with their start and end apart: 1 -> 1, of which waited for: 1 -> 1; matrix products, arithmetic and copies ran while one was open for 0% -> 0% of each run, Pallas kernels for 0% -> 3%
where the time goes in v3:
time: 36 us; the launch traced here: 35.8 us
  blocking collectives  27.8 us (77%)
  Pallas kernels  6.95 us (19%)
  between operations  0.69 us (2%)
    all_to_all x1, blocking collectives, local(): mine = swap(pack(query, keys, values, grad_out))  16.1 us
    all_to_all x1, blocking collectives, local(): return unpack(swap(given), query.shape[0])  11.7 us
    pallas_call x1, Pallas kernels, attend(): pl.pallas_call(functools.partial(finish_kernel, shares), out_shape=pltpu....  3.79 us
    pallas_call x1, Pallas kernels, attend(): pl.pallas_call(functools.partial(begin_kernel, shares), out_shape=(pltpu....  1.24 us
    pallas_call x1, Pallas kernels, pack(): pl.pallas_call(pack_kernel, out_shape=pltpu.VMEM((width // HD, 2 * rows,...  1.07 us
    pallas_call x1, Pallas kernels, unpack(): pl.pallas_call(unpack_kernel, out_shape=(shape,) * 3, in_specs=[VMEM], ou...  0.85 us
  transfers between devices with their start and end apart: 1, of which 1 were waited for; matrix products, arithmetic and copies ran while one was open for 0% of the time, Pallas kernels for 3%

profile of v3, /device:TPU:0, one launch (start us, length us, event | category | flops | bytes accessed | tf_op | source)
XLA Modules:
  0.0 35.8 jit_solution(7901421313726344079)
XLA Ops:
  0.6 1.1 %pack_heads.1 = bf16[8,128,128]{2,1,0:T(8,128)(2,1)S(1)} custom-call(bf16[64,512]{1,0:T(8,128)(2,1)} %q_ref.1, bf16[64,512]{1,0:T(8,128)(2,1)} %k_ref.1, bf16[64,512]{1,0:T(8,128)(2,1)} %v_ref.1, bf16[64,512]{1,0:T(8,128)(2,1)} %g_ref.1), custom_call_target="tpu_custom_call" | custom-call | tf_op jit(solution)/shard_map/pack_heads/pallas_call | solution.py:42
  1.7 0.0 copy-start
  1.7 0.0 copy-start.1
  1.7 0.0 copy-start.2
  1.7 16.1 %all_to_all.10.mine_ref.refs_0_ = bf16[8,128,128]{2,1,0:T(8,128)(2,1)S(1)} all-to-all(bf16[8,128,128]{2,1,0:T(8,128)(2,1)S(1)} %pack_heads.1), channel_id=1, replica_groups=mesh['grp'=2,'blk'=4,'head'=4] {'blk','head':(1)2}, dimensions={0} | all-to-all | bytes 524288 | tf_op jit(solution)/shard_map/all_to_all | solution.py:297
  17.8 0.0 collective-permute-start
  17.8 0.0 copy-done
  17.8 0.0 copy-done.1
  17.9 0.0 copy-done.2
  17.9 1.2 %attend_begin.1 = (bf16[1024,128]{1,0:T(8,128)(2,1)S(1)}, bf16[1024,128]{1,0:T(8,128)(2,1)S(1)}, bf16[4,256,256]{2,1,0:T(8,128)(2,1)S(1)}, bf16[128,512]{1,0:T(8...) custom-call(bf16[8,128,128]{2,1,0:T(8,128)(2,1)S(1)} %all_to_all.10.mine_ref.re, ...), custom_call_target="tpu_custom_call" | custom-call | flops 268435456 | bytes 2097152 | tf_op jit(solution)/shard_map/attend_begin/pallas_call | solution.py:230
  19.1 0.3 collective-permute-done.refs_1_
  19.4 3.8 %attend_finish.1 = bf16[8,96,128]{2,1,0:T(8,128)(2,1)S(1)} custom-call(bf16[8,128,128]{2,1,0:T(8,128)(2,1)S(1)} %all_to_all.10.mine_ref.refs_0_, bf16[8,128,128]{2,1,0:T(8,128)(2,1)S(1)} %collective-permute-done.refs_1_, bf16[1024,128]{1,0:T(8,128)(2,1)S(1)} %get-tuple-element.10.refs_2_, bf16[1024,128]{1,0:T(8,128)(2,1)S(1)} %get-tuple-element.11.refs_3_, ...), custom_call_target="tpu_custom_call" | custom-call | tf_op jit(solution)/shard_map/attend_finish/pallas_call | solution.py:250
  23.2 11.7 %all_to_all.11.in_ref = bf16[8,96,128]{2,1,0:T(8,128)(2,1)S(1)} all-to-all(bf16[8,96,128]{2,1,0:T(8,128)(2,1)S(1)} %attend_finish.1), channel_id=1, replica_groups=mesh['grp'=2,'blk'=4,'head'=4] {'blk','head':(1)2}, dimensions={0} | all-to-all | bytes 393216 | tf_op jit(solution)/shard_map/all_to_all | solution.py:303
  34.9 0.9 %unpack_heads.1 = (f32[64,512]{1,0:T(8,128)}, f32[64,512]{1,0:T(8,128)}, f32[64,512]{1,0:T(8,128)}) custom-call(bf16[8,96,128]{2,1,0:T(8,128)(2,1)S(1)} %all_to_all.11.in_ref), custom_call_target="tpu_custom_call" | custom-call | tf_op jit(solution)/shard_map/unpack_heads/pallas_call | solution.py:283
Async XLA Ops:
  1.7 16.1 %copy-start = (s32[32]{0:T(128)S(1)}, s32[32]{0:T(128)}, u32[]{:S(2)}) copy-start(s32[32]{0:T(128)} %valid_ref.1) | copy-start | bytes 388
  1.7 16.1 %copy-start.1 = (s32[32]{0:T(128)S(1)}, s32[32]{0:T(128)}, u32[]{:S(2)}) copy-start(s32[32]{0:T(128)} %views_ref.1) | copy-start | bytes 388
  1.7 16.1 %copy-start.2 = (f32[8]{0:T(128)S(1)}, f32[8]{0:T(128)}, u32[]{:S(2)}) copy-start(f32[8]{0:T(128)} %bias_ref.1) | copy-start | bytes 100
  17.8 1.5 %collective-permute-start = (bf16[8,128,128]{2,1,0:T(8,128)(2,1)S(1)}, bf16[8,128,128]{2,1,0:T(8,128)(2,1)S(1)}, u32[]{:S(2)}, u32[]{:S(2)}) collective-permute-start(bf16[8,128,128]{2,1,0:T(8,128)(2,1)S(1)} %all_to_all.10.mine_ref.refs_0_), channel_id=1, source_target_pairs={{1,0},{0,1},{3,2},{2,3},{5,4},{4,5},{7,6},{6,7},{9,8},{8,9},{11,10... | collective-permute-start | bytes 786440 | tf_op jit(solution)/shard_map/ppermute | solution.py:299

commit v4 on v2

--- a/solution.py
+++ b/solution.py
@@ -11,9 +11,9 @@
 HD = 64
 FRAME = 32
 PAIR = 2 * HD
-TILE = 128
-CHUNK = 128
-UNROLL = 4
+TILE = 256
+CHUNK = 64
+UNROLL = 2
 
 SCALE = 0.125
 DEAD = -1e30

time: 35.6 us -> 35.9 us (level)
  no operation moved by 1% of the time
where the time goes in v4:
time: 35.9 us; the launch traced here: 35.7 us
  blocking collectives  27.7 us (77%)
  Pallas kernels  5.71 us (16%)
  waiting for transfers between devices  1.53 us (4%)
  between operations  0.68 us (2%)
    all_to_all x1, blocking collectives, local(): mine = swap(pack(query, keys, values, grad_out))  16.1 us
    all_to_all x1, blocking collectives, local(): swap(attend(blocks, valid, views, cross_bias))  11.6 us
    pallas_call x1, Pallas kernels, attend(): pl.pallas_call(functools.partial(attend_kernel, len(blocks)), out_shape=j...  3.79 us
    ppermute x1, waiting for transfers between devices, local(): lax.ppermute(mine, 'share', [((i + k) % shares, i) for i in range(shares)])  1.53 us
    pallas_call x1, Pallas kernels, pack(): pl.pallas_call(pack_kernel, out_shape=pltpu.VMEM((width // HD, 2 * rows,...  1.07 us
    pallas_call x1, Pallas kernels, unpack(): pl.pallas_call(unpack_kernel, out_shape=(shape,) * 3, in_specs=[VMEM], ou...  0.85 us
  transfers between devices with their start and end apart: 1, of which 1 were waited for; matrix products, arithmetic and copies ran while one was open for 0% of the time, Pallas kernels for 0%

profile of v4, /device:TPU:0, one launch (start us, length us, event | category | flops | bytes accessed | tf_op | source)
XLA Modules:
  0.0 35.7 jit_solution(13785018276789398985)
XLA Ops:
  0.6 1.1 %pack_heads.1 = bf16[8,128,128]{2,1,0:T(8,128)(2,1)S(1)} custom-call(bf16[64,512]{1,0:T(8,128)(2,1)} %q_ref.1, bf16[64,512]{1,0:T(8,128)(2,1)} %k_ref.1, bf16[64,512]{1,0:T(8,128)(2,1)} %v_ref.1, bf16[64,512]{1,0:T(8,128)(2,1)} %g_ref.1), custom_call_target="tpu_custom_call" | custom-call | tf_op jit(solution)/shard_map/pack_heads/pallas_call | solution.py:42
  1.7 0.0 copy-start
  1.7 0.0 copy-start.1
  1.7 0.0 copy-start.2
  1.7 16.1 %all_to_all.10.refs_0_ = bf16[8,128,128]{2,1,0:T(8,128)(2,1)S(1)} all-to-all(bf16[8,128,128]{2,1,0:T(8,128)(2,1)S(1)} %pack_heads.1), channel_id=1, replica_groups=mesh['grp'=2,'blk'=4,'head'=4] {'blk','head':(1)2}, dimensions={0} | all-to-all | bytes 524288 | tf_op jit(solution)/shard_map/all_to_all | solution.py:222
  17.8 0.0 collective-permute-start
  17.8 1.5 %collective-permute-done.refs_1_ = bf16[8,128,128]{2,1,0:T(8,128)(2,1)S(1)} collective-permute-done((bf16[8,128,128]{2,1,0:T(8,128)(2,1)S(1)}, bf16[8,128,128]{2,1,0:T(8,128)(2,1)S(1)}, u32[]{:S(2)}, u32[]{:S(2)}) %collective-permute-start) | collective-permute-done | bytes 262176 | tf_op jit(solution)/shard_map/ppermute | solution.py:224
  19.4 0.0 copy-done
  19.4 0.0 copy-done.1
  19.4 0.0 copy-done.2
  19.4 3.8 %attend_backward.1 = bf16[8,96,128]{2,1,0:T(8,128)(2,1)S(1)} custom-call(bf16[8,128,128]{2,1,0:T(8,128)(2,1)S(1)} %all_to_all.10.refs_0_, bf16[8,128,128]{2,1,0:T(8,128)(2,1)S(1)} %collective-permute-done.refs_1_, s32[32]{0:T(128)S(1)} %copy-done, s32[32]{0:T(128)S(1)} %copy-done.1, f32[8]{0:T(128)S(1)} %copy-done.2), custom_call_target="tpu_custom_call" | custom-call | tf_op jit(solution)/shard_map/attend_backward/pallas_call | solution.py:175
  23.2 11.6 %all_to_all.11.in_ref = bf16[8,96,128]{2,1,0:T(8,128)(2,1)S(1)} all-to-all(bf16[8,96,128]{2,1,0:T(8,128)(2,1)S(1)} %attend_backward.1), channel_id=1, replica_groups=mesh['grp'=2,'blk'=4,'head'=4] {'blk','head':(1)2}, dimensions={0} | all-to-all | bytes 393216 | tf_op jit(solution)/shard_map/all_to_all | solution.py:227
  34.8 0.9 %unpack_heads.1 = (f32[64,512]{1,0:T(8,128)}, f32[64,512]{1,0:T(8,128)}, f32[64,512]{1,0:T(8,128)}) custom-call(bf16[8,96,128]{2,1,0:T(8,128)(2,1)S(1)} %all_to_all.11.in_ref), custom_call_target="tpu_custom_call" | custom-call | tf_op jit(solution)/shard_map/unpack_heads/pallas_call | solution.py:208
Async XLA Ops:
  1.7 17.7 %copy-start = (s32[32]{0:T(128)S(1)}, s32[32]{0:T(128)}, u32[]{:S(2)}) copy-start(s32[32]{0:T(128)} %refs_2_.1) | copy-start | bytes 388
  1.7 17.7 %copy-start.1 = (s32[32]{0:T(128)S(1)}, s32[32]{0:T(128)}, u32[]{:S(2)}) copy-start(s32[32]{0:T(128)} %refs_3_.1) | copy-start | bytes 388
  1.7 17.7 %copy-start.2 = (f32[8]{0:T(128)S(1)}, f32[8]{0:T(128)}, u32[]{:S(2)}) copy-start(f32[8]{0:T(128)} %refs_4_.1) | copy-start | bytes 100
  17.8 1.5 %collective-permute-start = (bf16[8,128,128]{2,1,0:T(8,128)(2,1)S(1)}, bf16[8,128,128]{2,1,0:T(8,128)(2,1)S(1)}, u32[]{:S(2)}, u32[]{:S(2)}) collective-permute-start(bf16[8,128,128]{2,1,0:T(8,128)(2,1)S(1)} %all_to_all.10.refs_0_), channel_id=1, source_target_pairs={{1,0},{0,1},{3,2},{2,3},{5,4},{4,5},{7,6},{6,7},{9,8},{8,9},{11,10... | collective-permute-start | bytes 786440 | tf_op jit(solution)/shard_map/ppermute | solution.py:224

commit v5 on v2

--- a/solution.py
+++ b/solution.py
@@ -13,7 +13,8 @@
 PAIR = 2 * HD
 TILE = 128
 CHUNK = 128
-UNROLL = 4
+SUBLANES = 8
+UNROLL = 2
 
 SCALE = 0.125
 DEAD = -1e30
@@ -92,7 +93,8 @@
                 )
                 kv_ref[here, PAIR:] = jnp.where(lane == 6, gone, marks).astype(jnp.bfloat16)
         here = slice(start, start + own)
-        flip_ref[:, here] = kv_ref[here, :PAIR].astype(jnp.float32).T.astype(jnp.bfloat16)
+        flip = kv_ref[here, :PAIR].astype(jnp.float32).T
+        flip_ref[:, here] = flip[:HD].astype(jnp.bfloat16)
 
     sum_ref[...] = jnp.zeros_like(sum_ref)
     low = lax.broadcasted_iota(jnp.int32, (TILE, PAIR), 1) < HD
@@ -119,46 +121,52 @@
             contract_last,
             preferred_element_type=jnp.float32,
         )
-        tops, totals, mixes, expos = [], [], [], []
+        tops, totals, mixes, expos, gws = [], [], [], [], []
         for c in range(chunks):
             at = slice(c * CHUNK, (c + 1) * CHUNK)
-            top = jnp.max(both[at, :TILE], axis=0, keepdims=True)
-            expo = jnp.exp2((both[at, :TILE] - top) * (SCALE * LOG2E))
+            raw = both[at, :TILE].reshape(-1, SUBLANES, TILE)
+            gw = both[at, TILE:].reshape(-1, SUBLANES, TILE)
+            top = jnp.max(raw, axis=0)
+            expo = jnp.exp2((raw - top) * (SCALE * LOG2E))
             expos.append(expo)
+            gws.append(gw)
             tops.append(top)
-            totals.append(jnp.sum(expo, axis=0, keepdims=True))
-            mixes.append(jnp.sum(expo * both[at, TILE:], axis=0, keepdims=True))
-        highest = functools.reduce(jnp.maximum, tops)
+            totals.append(jnp.sum(expo, axis=0))
+            mixes.append(jnp.sum(expo * gw, axis=0))
+        highest = jnp.max(functools.reduce(jnp.maximum, tops), axis=0, keepdims=True)
         factors = [jnp.exp2((top - highest) * (SCALE * LOG2E)) for top in tops]
-        inverse = 1.0 / sum(f * t for f, t in zip(factors, totals))
-        delta = sum(f * m for f, m in zip(factors, mixes)) * inverse
+        total = jnp.sum(sum(f * t for f, t in zip(factors, totals)), axis=0, keepdims=True)
+        mixed = jnp.sum(sum(f * m for f, m in zip(factors, mixes)), axis=0, keepdims=True)
+        inverse = 1.0 / total
+        delta = mixed * inverse
 
         lows, grads = [], []
         for c in range(chunks if ours else own_chunks):
-            at = slice(c * CHUNK, (c + 1) * CHUNK)
             weight = expos[c] * (factors[c] * inverse)
-            grads.append(
-                ((weight * SCALE) * (both[at, TILE:] - delta)).astype(jnp.bfloat16)
-            )
+            grad = (weight * SCALE) * (gws[c] - delta)
+            grads.append(grad.reshape(CHUNK, TILE).astype(jnp.bfloat16))
             if c < own_chunks:
-                lows.append(weight.astype(jnp.bfloat16))
+                lows.append(weight.reshape(CHUNK, TILE).astype(jnp.bfloat16))
+        return weights, jnp.concatenate(grads, axis=0), jnp.concatenate(lows, axis=0)
+
+    def two_tiles(ours, pair):
+        weights, grads, lows = zip(*(tile(ours, 2 * pair + which) for which in range(2)))
+        factors = [x for both in zip(grads, lows) for x in (both[0][:own], both[1])]
         sum_ref[...] += jnp.dot(
-            side_by_side(
-                jnp.concatenate(grads[:own_chunks], axis=0), jnp.concatenate(lows, axis=0)
-            ),
-            weights,
+            jnp.concatenate(factors, axis=1),
+            jnp.concatenate(weights, axis=0),
             preferred_element_type=jnp.float32,
         )
         if ours:
             turned = jnp.dot(
-                flip_ref[...],
-                jnp.concatenate(grads, axis=0),
-                preferred_element_type=jnp.float32,
+                flip_ref[...], side_by_side(*grads), preferred_element_type=jnp.float32
             )
-            dq_ref[here, :] = turned.T
-
-    pl.loop(0, tiles, unroll=unroll)(functools.partial(tile, True))
-    pl.loop(tiles, tiles * shares, unroll=unroll)(functools.partial(tile, False))
+            here = pl.ds(pl.multiple_of(pair * (2 * TILE), 2 * TILE), 2 * TILE)
+            dq_ref[here, :] = jnp.concatenate([turned, turned], axis=0).T
+
+    pairs = tiles // 2
+    pl.loop(0, pairs, unroll=unroll)(functools.partial(two_tiles, True))
+    pl.loop(pairs, pairs * shares, unroll=unroll)(functools.partial(two_tiles, False))
     out_ref[:, :rows, :] = sum_ref[...].astype(jnp.bfloat16).reshape(homes, rows, PAIR)
     for home in range(homes):
         start, half = home * rows, rows // 2
@@ -180,7 +188,7 @@
         scratch_shapes=[
             pltpu.VMEM((tokens, 2 * PAIR), jnp.bfloat16),
             pltpu.VMEM((tokens, PAIR), jnp.bfloat16),
-            pltpu.VMEM((PAIR, tokens), jnp.bfloat16),
+            pltpu.VMEM((HD, tokens), jnp.bfloat16),
             pltpu.VMEM((own, PAIR), jnp.float32),
             pltpu.VMEM((own, PAIR), jnp.float32),
         ],

time: 35.6 us -> 35.6 us (level)
  no operation moved by 1% of the time
where the time goes in v5:
time: 35.6 us; the launch traced here: 35.4 us
  blocking collectives  27.7 us (78%)
  Pallas kernels  5.43 us (15%)
  waiting for transfers between devices  1.53 us (4%)
  between operations  0.68 us (2%)
    all_to_all x1, blocking collectives, local(): mine = swap(pack(query, keys, values, grad_out))  16.1 us
    all_to_all x1, blocking collectives, local(): swap(attend(blocks, valid, views, cross_bias))  11.6 us
    pallas_call x1, Pallas kernels, attend(): pl.pallas_call(functools.partial(attend_kernel, len(blocks)), out_shape=j...  3.5 us
    ppermute x1, waiting for transfers between devices, local(): lax.ppermute(mine, 'share', [((i + k) % shares, i) for i in range(shares)])  1.53 us
    pallas_call x1, Pallas kernels, pack(): pl.pallas_call(pack_kernel, out_shape=pltpu.VMEM((width // HD, 2 * rows,...  1.07 us
    pallas_call x1, Pallas kernels, unpack(): pl.pallas_call(unpack_kernel, out_shape=(shape,) * 3, in_specs=[VMEM], ou...  0.85 us
  transfers between devices with their start and end apart: 1, of which 1 were waited for; matrix products, arithmetic and copies ran while one was open for 0% of the time, Pallas kernels for 0%

profile of v5, /device:TPU:0, one launch (start us, length us, event | category | flops | bytes accessed | tf_op | source)
XLA Modules:
  0.0 35.4 jit_solution(8962990745311473044)
XLA Ops:
  0.6 1.1 %pack_heads.1 = bf16[8,128,128]{2,1,0:T(8,128)(2,1)S(1)} custom-call(bf16[64,512]{1,0:T(8,128)(2,1)} %q_ref.1, bf16[64,512]{1,0:T(8,128)(2,1)} %k_ref.1, bf16[64,512]{1,0:T(8,128)(2,1)} %v_ref.1, bf16[64,512]{1,0:T(8,128)(2,1)} %g_ref.1), custom_call_target="tpu_custom_call" | custom-call | tf_op jit(solution)/shard_map/pack_heads/pallas_call | solution.py:43
  1.7 0.0 copy-start
  1.7 0.0 copy-start.1
  1.7 0.0 copy-start.2
  1.7 16.1 %all_to_all.10.refs_0_ = bf16[8,128,128]{2,1,0:T(8,128)(2,1)S(1)} all-to-all(bf16[8,128,128]{2,1,0:T(8,128)(2,1)S(1)} %pack_heads.1), channel_id=1, replica_groups=mesh['grp'=2,'blk'=4,'head'=4] {'blk','head':(1)2}, dimensions={0} | all-to-all | bytes 524288 | tf_op jit(solution)/shard_map/all_to_all | solution.py:230
  17.8 0.0 collective-permute-start
  17.8 1.5 %collective-permute-done.refs_1_ = bf16[8,128,128]{2,1,0:T(8,128)(2,1)S(1)} collective-permute-done((bf16[8,128,128]{2,1,0:T(8,128)(2,1)S(1)}, bf16[8,128,128]{2,1,0:T(8,128)(2,1)S(1)}, u32[]{:S(2)}, u32[]{:S(2)}) %collective-permute-start) | collective-permute-done | bytes 262176 | tf_op jit(solution)/shard_map/ppermute | solution.py:232
  19.4 0.0 copy-done
  19.4 0.0 copy-done.1
  19.4 0.0 copy-done.2
  19.4 3.5 %attend_backward.1 = bf16[8,96,128]{2,1,0:T(8,128)(2,1)S(1)} custom-call(bf16[8,128,128]{2,1,0:T(8,128)(2,1)S(1)} %all_to_all.10.refs_0_, bf16[8,128,128]{2,1,0:T(8,128)(2,1)S(1)} %collective-permute-done.refs_1_, s32[32]{0:T(128)S(1)} %copy-done, s32[32]{0:T(128)S(1)} %copy-done.1, f32[8]{0:T(128)S(1)} %copy-done.2), custom_call_target="tpu_custom_call" | custom-call | tf_op jit(solution)/shard_map/attend_backward/pallas_call | solution.py:183
  22.9 11.6 %all_to_all.11.in_ref = bf16[8,96,128]{2,1,0:T(8,128)(2,1)S(1)} all-to-all(bf16[8,96,128]{2,1,0:T(8,128)(2,1)S(1)} %attend_backward.1), channel_id=1, replica_groups=mesh['grp'=2,'blk'=4,'head'=4] {'blk','head':(1)2}, dimensions={0} | all-to-all | bytes 393216 | tf_op jit(solution)/shard_map/all_to_all | solution.py:235
  34.5 0.9 %unpack_heads.1 = (f32[64,512]{1,0:T(8,128)}, f32[64,512]{1,0:T(8,128)}, f32[64,512]{1,0:T(8,128)}) custom-call(bf16[8,96,128]{2,1,0:T(8,128)(2,1)S(1)} %all_to_all.11.in_ref), custom_call_target="tpu_custom_call" | custom-call | tf_op jit(solution)/shard_map/unpack_heads/pallas_call | solution.py:216
Async XLA Ops:
  1.7 17.7 %copy-start = (s32[32]{0:T(128)S(1)}, s32[32]{0:T(128)}, u32[]{:S(2)}) copy-start(s32[32]{0:T(128)} %refs_2_.1) | copy-start | bytes 388
  1.7 17.7 %copy-start.1 = (s32[32]{0:T(128)S(1)}, s32[32]{0:T(128)}, u32[]{:S(2)}) copy-start(s32[32]{0:T(128)} %refs_3_.1) | copy-start | bytes 388
  1.7 17.7 %copy-start.2 = (f32[8]{0:T(128)S(1)}, f32[8]{0:T(128)}, u32[]{:S(2)}) copy-start(f32[8]{0:T(128)} %refs_4_.1) | copy-start | bytes 100
  17.8 1.5 %collective-permute-start = (bf16[8,128,128]{2,1,0:T(8,128)(2,1)S(1)}, bf16[8,128,128]{2,1,0:T(8,128)(2,1)S(1)}, u32[]{:S(2)}, u32[]{:S(2)}) collective-permute-start(bf16[8,128,128]{2,1,0:T(8,128)(2,1)S(1)} %all_to_all.10.refs_0_), channel_id=1, source_target_pairs={{1,0},{0,1},{3,2},{2,3},{5,4},{4,5},{7,6},{6,7},{9,8},{8,9},{11,10... | collective-permute-start | bytes 786440 | tf_op jit(solution)/shard_map/ppermute | solution.py:232

commit v6 on v5

--- a/solution.py
+++ b/solution.py
@@ -14,7 +14,6 @@
 TILE = 128
 CHUNK = 128
 SUBLANES = 8
-UNROLL = 2
 
 SCALE = 0.125
 DEAD = -1e30
@@ -59,7 +58,6 @@
     per_home, per_tile = rows // FRAME, TILE // rows
     tiles, chunks, own_chunks = own // TILE, tokens // CHUNK, own // CHUNK
     mine = lax.axis_index("share")
-    unroll = UNROLL if shares <= 2 else 1
     slot = lax.broadcasted_iota(jnp.int32, (FRAME, PAIR), 0)
     lane = lax.broadcasted_iota(jnp.int32, (1, PAIR), 1)
 
@@ -100,7 +98,7 @@
     low = lax.broadcasted_iota(jnp.int32, (TILE, PAIR), 1) < HD
     contract_last = (((1,), (1,)), ((), ()))
 
-    def tile(ours, index):
+    def score(index):
         here = pl.ds(pl.multiple_of(index * TILE, TILE), TILE)
         qg = qg_ref[here, :].astype(jnp.float32)
         weights = jnp.concatenate(
@@ -114,32 +112,32 @@
             marks.append(jnp.broadcast_to(row, (FRAME, PAIR)))
         marks.append(jnp.zeros((TILE, PAIR), jnp.float32))
         marks = jnp.concatenate(marks, axis=0).astype(jnp.bfloat16)
-
-        both = lax.dot_general(
+        return weights, lax.dot_general(
             kv_ref[...],
             side_by_side(weights, marks),
             contract_last,
             preferred_element_type=jnp.float32,
         )
-        tops, totals, mixes, expos, gws = [], [], [], [], []
+
+    def exponentials(both):
+        parts = []
         for c in range(chunks):
             at = slice(c * CHUNK, (c + 1) * CHUNK)
             raw = both[at, :TILE].reshape(-1, SUBLANES, TILE)
             gw = both[at, TILE:].reshape(-1, SUBLANES, TILE)
             top = jnp.max(raw, axis=0)
             expo = jnp.exp2((raw - top) * (SCALE * LOG2E))
-            expos.append(expo)
-            gws.append(gw)
-            tops.append(top)
-            totals.append(jnp.sum(expo, axis=0))
-            mixes.append(jnp.sum(expo * gw, axis=0))
+            parts.append((expo, gw, top, jnp.sum(expo, axis=0), jnp.sum(expo * gw, axis=0)))
+        return parts
+
+    def gradients(ours, parts):
+        expos, gws, tops, totals, mixes = zip(*parts)
         highest = jnp.max(functools.reduce(jnp.maximum, tops), axis=0, keepdims=True)
         factors = [jnp.exp2((top - highest) * (SCALE * LOG2E)) for top in tops]
         total = jnp.sum(sum(f * t for f, t in zip(factors, totals)), axis=0, keepdims=True)
         mixed = jnp.sum(sum(f * m for f, m in zip(factors, mixes)), axis=0, keepdims=True)
         inverse = 1.0 / total
         delta = mixed * inverse
-
         lows, grads = [], []
         for c in range(chunks if ours else own_chunks):
             weight = expos[c] * (factors[c] * inverse)
@@ -147,10 +145,10 @@
             grads.append(grad.reshape(CHUNK, TILE).astype(jnp.bfloat16))
             if c < own_chunks:
                 lows.append(weight.reshape(CHUNK, TILE).astype(jnp.bfloat16))
-        return weights, jnp.concatenate(grads, axis=0), jnp.concatenate(lows, axis=0)
-
-    def two_tiles(ours, pair):
-        weights, grads, lows = zip(*(tile(ours, 2 * pair + which) for which in range(2)))
+        return jnp.concatenate(grads, axis=0), jnp.concatenate(lows, axis=0)
+
+    def leave(ours, first, pair):
+        weights, grads, lows = zip(*pair)
         factors = [x for both in zip(grads, lows) for x in (both[0][:own], both[1])]
         sum_ref[...] += jnp.dot(
             jnp.concatenate(factors, axis=1),
@@ -161,12 +159,31 @@
             turned = jnp.dot(
                 flip_ref[...], side_by_side(*grads), preferred_element_type=jnp.float32
             )
-            here = pl.ds(pl.multiple_of(pair * (2 * TILE), 2 * TILE), 2 * TILE)
+            here = pl.ds(pl.multiple_of(first * TILE, 2 * TILE), 2 * TILE)
             dq_ref[here, :] = jnp.concatenate([turned, turned], axis=0).T
 
-    pairs = tiles // 2
-    pl.loop(0, pairs, unroll=unroll)(functools.partial(two_tiles, True))
-    pl.loop(pairs, pairs * shares, unroll=unroll)(functools.partial(two_tiles, False))
+    def pipeline(work):
+        scored, expos, done = {}, {}, {}
+        for step in range(len(work) + 2):
+            if step < len(work):
+                scored[step] = score(work[step][1])
+            if 0 <= step - 1 < len(work):
+                weights, both = scored.pop(step - 1)
+                expos[step - 1] = weights, exponentials(both)
+            if 0 <= step - 2:
+                ours, index = work[step - 2]
+                weights, parts = expos.pop(step - 2)
+                done[step - 2] = (weights, *gradients(ours, parts))
+                if step % 2:
+                    leave(ours, work[step - 3][1], (done.pop(step - 3), done.pop(step - 2)))
+
+    if shares <= 2:
+        pipeline([(index < tiles, index) for index in range(tiles * shares)])
+    else:
+        pl.loop(0, tiles, step=2)(lambda i: pipeline([(True, i), (True, i + 1)]))
+        pl.loop(tiles, tiles * shares, step=2)(
+            lambda i: pipeline([(False, i), (False, i + 1)])
+        )
     out_ref[:, :rows, :] = sum_ref[...].astype(jnp.bfloat16).reshape(homes, rows, PAIR)
     for home in range(homes):
         start, half = home * rows, rows // 2

time: 35.6 us -> 35.3 us (level)
  no operation moved by 1% of the time
where the time goes in v6:
time: 35.3 us; the launch traced here: 35.1 us
  blocking collectives  27.7 us (78%)
  Pallas kernels  5.12 us (15%)
  waiting for transfers between devices  1.53 us (4%)
  between operations  0.67 us (2%)
    all_to_all x1, blocking collectives, local(): mine = swap(pack(query, keys, values, grad_out))  16.1 us
    all_to_all x1, blocking collectives, local(): swap(attend(blocks, valid, views, cross_bias))  11.6 us
    pallas_call x1, Pallas kernels, attend(): pl.pallas_call(functools.partial(attend_kernel, len(blocks)), out_shape=j...  3.2 us
    ppermute x1, waiting for transfers between devices, local(): lax.ppermute(mine, 'share', [((i + k) % shares, i) for i in range(shares)])  1.53 us
    pallas_call x1, Pallas kernels, pack(): pl.pallas_call(pack_kernel, out_shape=pltpu.VMEM((width // HD, 2 * rows,...  1.07 us
    pallas_call x1, Pallas kernels, unpack(): pl.pallas_call(unpack_kernel, out_shape=(shape,) * 3, in_specs=[VMEM], ou...  0.85 us
  transfers between devices with their start and end apart: 1, of which 1 were waited for; matrix products, arithmetic and copies ran while one was open for 0% of the time, Pallas kernels for 0%

profile of v6, /device:TPU:0, one launch (start us, length us, event | category | flops | bytes accessed | tf_op | source)
XLA Modules:
  0.0 35.1 jit_solution(7061956892851163952)
XLA Ops:
  0.6 1.1 %pack_heads.1 = bf16[8,128,128]{2,1,0:T(8,128)(2,1)S(1)} custom-call(bf16[64,512]{1,0:T(8,128)(2,1)} %q_ref.1, bf16[64,512]{1,0:T(8,128)(2,1)} %k_ref.1, bf16[64,512]{1,0:T(8,128)(2,1)} %v_ref.1, bf16[64,512]{1,0:T(8,128)(2,1)} %g_ref.1), custom_call_target="tpu_custom_call" | custom-call | tf_op jit(solution)/shard_map/pack_heads/pallas_call | solution.py:42
  1.7 0.0 copy-start
  1.7 0.0 copy-start.1
  1.7 0.0 copy-start.2
  1.7 16.1 %all_to_all.10.refs_0_ = bf16[8,128,128]{2,1,0:T(8,128)(2,1)S(1)} all-to-all(bf16[8,128,128]{2,1,0:T(8,128)(2,1)S(1)} %pack_heads.1), channel_id=1, replica_groups=mesh['grp'=2,'blk'=4,'head'=4] {'blk','head':(1)2}, dimensions={0} | all-to-all | bytes 524288 | tf_op jit(solution)/shard_map/all_to_all | solution.py:247
  17.8 0.0 collective-permute-start
  17.8 1.5 %collective-permute-done.refs_1_ = bf16[8,128,128]{2,1,0:T(8,128)(2,1)S(1)} collective-permute-done((bf16[8,128,128]{2,1,0:T(8,128)(2,1)S(1)}, bf16[8,128,128]{2,1,0:T(8,128)(2,1)S(1)}, u32[]{:S(2)}, u32[]{:S(2)}) %collective-permute-start) | collective-permute-done | bytes 262176 | tf_op jit(solution)/shard_map/ppermute | solution.py:249
  19.4 0.0 copy-done
  19.4 0.0 copy-done.1
  19.4 0.0 copy-done.2
  19.4 3.2 %attend_backward.1 = bf16[8,96,128]{2,1,0:T(8,128)(2,1)S(1)} custom-call(bf16[8,128,128]{2,1,0:T(8,128)(2,1)S(1)} %all_to_all.10.refs_0_, bf16[8,128,128]{2,1,0:T(8,128)(2,1)S(1)} %collective-permute-done.refs_1_, s32[32]{0:T(128)S(1)} %copy-done, s32[32]{0:T(128)S(1)} %copy-done.1, f32[8]{0:T(128)S(1)} %copy-done.2), custom_call_target="tpu_custom_call" | custom-call | tf_op jit(solution)/shard_map/attend_backward/pallas_call | solution.py:200
  22.6 11.6 %all_to_all.11.in_ref = bf16[8,96,128]{2,1,0:T(8,128)(2,1)S(1)} all-to-all(bf16[8,96,128]{2,1,0:T(8,128)(2,1)S(1)} %attend_backward.1), channel_id=1, replica_groups=mesh['grp'=2,'blk'=4,'head'=4] {'blk','head':(1)2}, dimensions={0} | all-to-all | bytes 393216 | tf_op jit(solution)/shard_map/all_to_all | solution.py:252
  34.2 0.9 %unpack_heads.1 = (f32[64,512]{1,0:T(8,128)}, f32[64,512]{1,0:T(8,128)}, f32[64,512]{1,0:T(8,128)}) custom-call(bf16[8,96,128]{2,1,0:T(8,128)(2,1)S(1)} %all_to_all.11.in_ref), custom_call_target="tpu_custom_call" | custom-call | tf_op jit(solution)/shard_map/unpack_heads/pallas_call | solution.py:233
Async XLA Ops:
  1.7 17.7 %copy-start = (s32[32]{0:T(128)S(1)}, s32[32]{0:T(128)}, u32[]{:S(2)}) copy-start(s32[32]{0:T(128)} %refs_2_.1) | copy-start | bytes 388
  1.7 17.7 %copy-start.1 = (s32[32]{0:T(128)S(1)}, s32[32]{0:T(128)}, u32[]{:S(2)}) copy-start(s32[32]{0:T(128)} %refs_3_.1) | copy-start | bytes 388
  1.7 17.7 %copy-start.2 = (f32[8]{0:T(128)S(1)}, f32[8]{0:T(128)}, u32[]{:S(2)}) copy-start(f32[8]{0:T(128)} %refs_4_.1) | copy-start | bytes 100
  17.8 1.5 %collective-permute-start = (bf16[8,128,128]{2,1,0:T(8,128)(2,1)S(1)}, bf16[8,128,128]{2,1,0:T(8,128)(2,1)S(1)}, u32[]{:S(2)}, u32[]{:S(2)}) collective-permute-start(bf16[8,128,128]{2,1,0:T(8,128)(2,1)S(1)} %all_to_all.10.refs_0_), channel_id=1, source_target_pairs={{1,0},{0,1},{3,2},{2,3},{5,4},{4,5},{7,6},{6,7},{9,8},{8,9},{11,10... | collective-permute-start | bytes 786440 | tf_op jit(solution)/shard_map/ppermute | solution.py:249

commit v7 on v3

--- a/solution.py
+++ b/solution.py
@@ -13,7 +13,7 @@
 PAIR = 2 * HD
 TILE = 128
 CHUNK = 128
-UNROLL = 4
+SUBLANES = 8
 
 SCALE = 0.125
 DEAD = -1e30
@@ -68,10 +68,10 @@
 
 
 def exponentials(raw, gw):
-    top = jnp.max(raw, axis=0, keepdims=True)
+    raw, gw = (x.reshape(-1, SUBLANES, TILE) for x in (raw, gw))
+    top = jnp.max(raw, axis=0)
     expo = jnp.exp2((raw - top) * (SCALE * LOG2E))
-    total = jnp.sum(expo, axis=0, keepdims=True)
-    return expo, (top, total, jnp.sum(expo * gw, axis=0, keepdims=True))
+    return expo, (top, jnp.sum(expo, axis=0), jnp.sum(expo * gw, axis=0))
 
 
 def chunk_of(c):
@@ -83,7 +83,6 @@
     homes, rows = mine_ref.shape[0], mine_ref.shape[1] // 2
     own = homes * rows
     per_home, per_tile, tiles = rows // FRAME, TILE // rows, own // TILE
-    unroll = UNROLL if shares <= 2 else 1
     slot = lax.broadcasted_iota(jnp.int32, (FRAME, PAIR), 0)
     lane = lax.broadcasted_iota(jnp.int32, (1, PAIR), 1)
 
@@ -112,28 +111,33 @@
                 ).astype(jnp.bfloat16)
 
     kv = mine_ref[:, :rows, :].reshape(own, PAIR)
-    flip_ref[...] = kv.astype(jnp.float32).T.astype(jnp.bfloat16)
+    flip_ref[...] = kv.astype(jnp.float32).T[:HD].astype(jnp.bfloat16)
     keys_ref[:, :PAIR] = kv
     keys_ref[:, PAIR:] = key_mark_ref[:own, :]
 
-    def tile(index):
-        qg = mine_ref[pl.ds(index * per_tile, per_tile), rows:, :].reshape(TILE, PAIR)
-        here = pl.ds(pl.multiple_of(index * TILE, TILE), TILE)
-        marks = query_mark_ref[here, :]
+    def score(index):
+        qg = mine_ref[index * per_tile : (index + 1) * per_tile, rows:, :].reshape(TILE, PAIR)
+        marks = query_mark_ref[index * TILE : (index + 1) * TILE, :]
         weights = side_by_side(
             query_weights(qg), jnp.concatenate([marks, jnp.zeros_like(marks)], axis=0)
         )
         weights_ref[index] = weights
-        both = products(keys_ref[...], weights)
+        return products(keys_ref[...], weights)
+
+    def leave(index, both):
         gw_ref[index] = both[:, TILE:]
         for c in range(own // CHUNK):
             at = chunk_of(c)
             expo, stats = exponentials(both[at, :TILE], both[at, TILE:])
-            expo_ref[index, at, :] = expo
+            expo_ref[index, at, :] = expo.reshape(CHUNK, TILE)
             for which, stat in enumerate(stats):
-                stat_ref[index, which, c : c + 1, :] = stat
-
-    pl.loop(0, tiles, unroll=unroll)(tile)
+                stat_ref[index, which, c] = stat
+
+    scored = None
+    for step in range(tiles + 1):
+        last, scored = scored, score(step) if step < tiles else None
+        if step:
+            leave(step - 1, last)
 
 
 def finish_kernel(shares, *refs):
@@ -144,75 +148,103 @@
     own = homes * rows
     tokens = own * shares
     tiles, chunks, own_chunks = own // TILE, tokens // CHUNK, own // CHUNK
-    unroll = UNROLL if shares <= 2 else 1
 
     keys_ref[:, PAIR:] = key_mark_ref[...]
+    flip_ref[:, :own] = own_flip_ref[...]
     for block in range(shares):
         here = slice(block * own, (block + 1) * own)
         kv = blocks[block][:, :rows, :].reshape(own, PAIR)
         keys_ref[here, :PAIR] = kv
         if block:
             there = slice((block - 1) * own, block * own)
-            flip_ref[:, there] = kv.astype(jnp.float32).T.astype(jnp.bfloat16)
+            flip_ref[:, here] = kv.astype(jnp.float32).T[:HD].astype(jnp.bfloat16)
             qg_ref[there, :] = blocks[block][:, rows:, :].reshape(own, PAIR)
     sum_ref[...] = jnp.zeros_like(sum_ref)
 
-    def tile(ours, index):
-        here = pl.ds(pl.multiple_of(index * TILE, TILE), TILE)
+    def score(ours, index):
         if ours:
             weights = weights_ref[index]
-            given = own_chunks
-            if chunks > own_chunks:
-                both = products(keys_ref[own:, :], weights)
-        else:
-            marks = query_mark_ref[pl.ds(pl.multiple_of(own + index * TILE, TILE), TILE), :]
-            weights = side_by_side(
-                query_weights(qg_ref[here, :]),
-                jnp.concatenate([marks, jnp.zeros_like(marks)], axis=0),
-            )
-            given = 0
-            both = products(keys_ref[...], weights)
-        expos, gws, stats = [], [], []
-        for c in range(chunks):
-            if c < given:
-                expos.append(expo_ref[index, chunk_of(c), :])
-                gws.append(gw_ref[index, chunk_of(c), :])
-                stats.append([stat_ref[index, which, c : c + 1, :] for which in range(3)])
-            else:
-                at = chunk_of(c - given)
-                gws.append(both[at, TILE:])
-                expo, stat = exponentials(both[at, :TILE], gws[-1])
-                expos.append(expo)
-                stats.append(stat)
-        highest = functools.reduce(jnp.maximum, [top for top, _, _ in stats])
-        factors = [jnp.exp2((top - highest) * (SCALE * LOG2E)) for top, _, _ in stats]
-        inverse = 1.0 / sum(f * total for f, (_, total, _) in zip(factors, stats))
-        delta = sum(f * mix for f, (_, _, mix) in zip(factors, stats)) * inverse
-
+            if chunks == own_chunks:
+                return weights, None
+            return weights, products(keys_ref[own:, :], weights)
+        here = pl.ds(pl.multiple_of(index * TILE, TILE), TILE)
+        there = pl.ds(pl.multiple_of(own + index * TILE, TILE), TILE)
+        marks = query_mark_ref[there, :]
+        weights = side_by_side(
+            query_weights(qg_ref[here, :]),
+            jnp.concatenate([marks, jnp.zeros_like(marks)], axis=0),
+        )
+        return weights, products(keys_ref[...], weights)
+
+    def all_exponentials(ours, index, both):
+        parts = []
+        given = own_chunks if ours else 0
+        for c in range(given):
+            parts.append((None, None, *(stat_ref[index, which, c] for which in range(3))))
+        for c in range(chunks - given):
+            gw = both[chunk_of(c), TILE:]
+            expo, stats = exponentials(both[chunk_of(c), :TILE], gw)
+            parts.append((expo, gw.reshape(-1, SUBLANES, TILE), *stats))
+        return parts
+
+    def gradients(ours, index, parts):
+        expos, gws, tops, totals, mixes = zip(*parts)
+        highest = jnp.max(functools.reduce(jnp.maximum, tops), axis=0, keepdims=True)
+        factors = [jnp.exp2((top - highest) * (SCALE * LOG2E)) for top in tops]
+        total = jnp.sum(sum(f * t for f, t in zip(factors, totals)), axis=0, keepdims=True)
+        mixed = jnp.sum(sum(f * m for f, m in zip(factors, mixes)), axis=0, keepdims=True)
+        inverse = 1.0 / total
+        delta = mixed * inverse
         lows, grads = [], []
         for c in range(chunks if ours else own_chunks):
-            weight = expos[c] * (factors[c] * inverse)
-            grads.append(((weight * SCALE) * (gws[c] - delta)).astype(jnp.bfloat16))
+            expo, gw = expos[c], gws[c]
+            if expo is None:
+                expo, gw = (
+                    ref[index, chunk_of(c), :].reshape(-1, SUBLANES, TILE)
+                    for ref in (expo_ref, gw_ref)
+                )
+            weight = expo * (factors[c] * inverse)
+            grad = (weight * SCALE) * (gw - delta)
+            grads.append(grad.reshape(CHUNK, TILE).astype(jnp.bfloat16))
             if c < own_chunks:
-                lows.append(weight.astype(jnp.bfloat16))
-        own_grads = jnp.concatenate(grads[:own_chunks], axis=0)
+                lows.append(weight.reshape(CHUNK, TILE).astype(jnp.bfloat16))
+        return jnp.concatenate(grads, axis=0), jnp.concatenate(lows, axis=0)
+
+    def leave(ours, first, pair):
+        weights, grads, lows = zip(*pair)
+        factors = [x for both in zip(grads, lows) for x in (both[0][:own], both[1])]
         sum_ref[...] += jnp.dot(
-            side_by_side(own_grads, jnp.concatenate(lows, axis=0)),
-            weights[:, :PAIR],
+            jnp.concatenate(factors, axis=1),
+            jnp.concatenate([each[:, :PAIR] for each in weights], axis=0),
             preferred_element_type=jnp.float32,
         )
         if ours:
-            turned = jnp.dot(own_flip_ref[...], own_grads, preferred_element_type=jnp.float32)
-            if chunks > own_chunks:
-                turned += jnp.dot(
-                    flip_ref[...],
-                    jnp.concatenate(grads[own_chunks:], axis=0),
-                    preferred_element_type=jnp.float32,
-                )
-            dq_ref[here, :] = turned.T
-
-    pl.loop(0, tiles, unroll=unroll)(functools.partial(tile, True))
-    pl.loop(0, tiles * (shares - 1), unroll=unroll)(functools.partial(tile, False))
+            turned = jnp.dot(
+                flip_ref[...], side_by_side(*grads), preferred_element_type=jnp.float32
+            )
+            here = pl.ds(pl.multiple_of(first * TILE, 2 * TILE), 2 * TILE)
+            dq_ref[here, :] = jnp.concatenate([turned, turned], axis=0).T
+
+    def pipeline(work):
+        scored, expos, done = {}, {}, {}
+        for step in range(len(work) + 2):
+            if step < len(work):
+                scored[step] = score(*work[step])
+            if 0 <= step - 1 < len(work):
+                weights, both = scored.pop(step - 1)
+                expos[step - 1] = weights, all_exponentials(*work[step - 1], both)
+            if 0 <= step - 2:
+                weights, parts = expos.pop(step - 2)
+                done[step - 2] = (weights, *gradients(*work[step - 2], parts))
+                if step % 2:
+                    leave(*work[step - 3], (done.pop(step - 3), done.pop(step - 2)))
+
+    others = tiles * (shares - 1)
+    if shares <= 2:
+        pipeline([(True, i) for i in range(tiles)] + [(False, i) for i in range(others)])
+    else:
+        pl.loop(0, tiles, step=2)(lambda i: pipeline([(True, i), (True, i + 1)]))
+        pl.loop(0, others, step=2)(lambda i: pipeline([(False, i), (False, i + 1)]))
     out_ref[:, :rows, :] = sum_ref[...].astype(jnp.bfloat16).reshape(homes, rows, PAIR)
     for home in range(homes):
         start, half = home * rows, rows // 2
@@ -233,10 +265,10 @@
             pltpu.VMEM((tokens, PAIR), jnp.bfloat16),
             pltpu.VMEM((tokens, PAIR), jnp.bfloat16),
             pltpu.VMEM((tiles, 2 * TILE, 2 * PAIR), jnp.bfloat16),
-            pltpu.VMEM((PAIR, own), jnp.bfloat16),
+            pltpu.VMEM((HD, own), jnp.bfloat16),
             pltpu.VMEM((tiles, own, TILE), jnp.float32),
             pltpu.VMEM((tiles, own, TILE), jnp.float32),
-            pltpu.VMEM((tiles, 3, own // CHUNK, TILE), jnp.float32),
+            pltpu.VMEM((tiles, 3, own // CHUNK, SUBLANES, TILE), jnp.float32),
         ),
         in_specs=[VMEM] + [SMEM] * 3,
         out_specs=(VMEM,) * 7,
@@ -255,7 +287,7 @@
         scratch_shapes=[
             pltpu.VMEM((tokens, 2 * PAIR), jnp.bfloat16),
             pltpu.VMEM((max(tokens - own, TILE), PAIR), jnp.bfloat16),
-            pltpu.VMEM((PAIR, max(tokens - own, TILE)), jnp.bfloat16),
+            pltpu.VMEM((HD, tokens), jnp.bfloat16),
             pltpu.VMEM((own, PAIR), jnp.float32),
             pltpu.VMEM((own, PAIR), jnp.float32),
         ],

time: 36 us -> 34.7 us (0.964)
  Pallas kernels: 6.95 us -> 5.61 us
    pallas_call x1, Pallas kernels: 3.79 us -> 2.49 us  [attend(): pl.pallas_call(functools.partial(finish_kernel, shares), out_shape=pltpu....]
where the time goes in v7:
time: 34.7 us; the launch traced here: 34.4 us
  blocking collectives  27.8 us (80%)
  Pallas kernels  5.61 us (16%)
  between operations  0.69 us (2%)
    all_to_all x1, blocking collectives, local(): mine = swap(pack(query, keys, values, grad_out))  16.1 us
    all_to_all x1, blocking collectives, local(): return unpack(swap(given), query.shape[0])  11.7 us
    pallas_call x1, Pallas kernels, attend(): pl.pallas_call(functools.partial(finish_kernel, shares), out_shape=pltpu....  2.49 us
    pallas_call x1, Pallas kernels, attend(): pl.pallas_call(functools.partial(begin_kernel, shares), out_shape=(pltpu....  1.2 us
    pallas_call x1, Pallas kernels, pack(): pl.pallas_call(pack_kernel, out_shape=pltpu.VMEM((width // HD, 2 * rows,...  1.07 us
    pallas_call x1, Pallas kernels, unpack(): pl.pallas_call(unpack_kernel, out_shape=(shape,) * 3, in_specs=[VMEM], ou...  0.85 us
  transfers between devices with their start and end apart: 1, of which 1 were waited for; matrix products, arithmetic and copies ran while one was open for 0% of the time, Pallas kernels for 3%

profile of v7, /device:TPU:0, one launch (start us, length us, event | category | flops | bytes accessed | tf_op | source)
XLA Modules:
  0.0 34.4 jit_solution(809134904729793201)
XLA Ops:
  0.6 1.1 %pack_heads.1 = bf16[8,128,128]{2,1,0:T(8,128)(2,1)S(1)} custom-call(bf16[64,512]{1,0:T(8,128)(2,1)} %q_ref.1, bf16[64,512]{1,0:T(8,128)(2,1)} %k_ref.1, bf16[64,512]{1,0:T(8,128)(2,1)} %v_ref.1, bf16[64,512]{1,0:T(8,128)(2,1)} %g_ref.1), custom_call_target="tpu_custom_call" | custom-call | tf_op jit(solution)/shard_map/pack_heads/pallas_call | solution.py:42
  1.7 0.0 copy-start
  1.7 0.0 copy-start.1
  1.7 0.0 copy-start.2
  1.7 16.1 %all_to_all.10.mine_ref.refs_0_ = bf16[8,128,128]{2,1,0:T(8,128)(2,1)S(1)} all-to-all(bf16[8,128,128]{2,1,0:T(8,128)(2,1)S(1)} %pack_heads.1), channel_id=1, replica_groups=mesh['grp'=2,'blk'=4,'head'=4] {'blk','head':(1)2}, dimensions={0} | all-to-all | bytes 524288 | tf_op jit(solution)/shard_map/all_to_all | solution.py:329
  17.8 0.0 collective-permute-start
  17.8 0.0 copy-done
  17.8 0.0 copy-done.1
  17.9 0.0 copy-done.2
  17.9 1.2 %attend_begin.1 = (bf16[1024,128]{1,0:T(8,128)(2,1)S(1)}, bf16[1024,128]{1,0:T(8,128)(2,1)S(1)}, bf16[4,256,256]{2,1,0:T(8,128)(2,1)S(1)}, bf16[64,512]{1,0:T(8,...) custom-call(bf16[8,128,128]{2,1,0:T(8,128)(2,1)S(1)} %all_to_all.10.mine_ref, ...), custom_call_target="tpu_custom_call" | custom-call | flops 268435456 | bytes 2097152 | tf_op jit(solution)/shard_map/attend_begin/pallas_call | solution.py:262
  19.1 0.3 collective-permute-done.refs_1_
  19.4 2.5 %attend_finish.1 = bf16[8,96,128]{2,1,0:T(8,128)(2,1)S(1)} custom-call(bf16[8,128,128]{2,1,0:T(8,128)(2,1)S(1)} %all_to_all.10.mine_ref.refs_0_, bf16[8,128,128]{2,1,0:T(8,128)(2,1)S(1)} %collective-permute-done.refs_1_, bf16[1024,128]{1,0:T(8,128)(2,1)S(1)} %get-tuple-element.10.refs_2_, bf16[1024,128]{1,0:T(8,128)(2,1)S(1)} %get-tuple-element.11.refs_3_, ...), custom_call_target="tpu_custom_call" | custom-call | tf_op jit(solution)/shard_map/attend_finish/pallas_call | solution.py:282
  21.9 11.7 %all_to_all.11.in_ref = bf16[8,96,128]{2,1,0:T(8,128)(2,1)S(1)} all-to-all(bf16[8,96,128]{2,1,0:T(8,128)(2,1)S(1)} %attend_finish.1), channel_id=1, replica_groups=mesh['grp'=2,'blk'=4,'head'=4] {'blk','head':(1)2}, dimensions={0} | all-to-all | bytes 393216 | tf_op jit(solution)/shard_map/all_to_all | solution.py:335
  33.6 0.9 %unpack_heads.1 = (f32[64,512]{1,0:T(8,128)}, f32[64,512]{1,0:T(8,128)}, f32[64,512]{1,0:T(8,128)}) custom-call(bf16[8,96,128]{2,1,0:T(8,128)(2,1)S(1)} %all_to_all.11.in_ref), custom_call_target="tpu_custom_call" | custom-call | tf_op jit(solution)/shard_map/unpack_heads/pallas_call | solution.py:315
Async XLA Ops:
  1.7 16.1 %copy-start = (s32[32]{0:T(128)S(1)}, s32[32]{0:T(128)}, u32[]{:S(2)}) copy-start(s32[32]{0:T(128)} %valid_ref.1) | copy-start | bytes 388
  1.7 16.1 %copy-start.1 = (s32[32]{0:T(128)S(1)}, s32[32]{0:T(128)}, u32[]{:S(2)}) copy-start(s32[32]{0:T(128)} %views_ref.1) | copy-start | bytes 388
  1.7 16.1 %copy-start.2 = (f32[8]{0:T(128)S(1)}, f32[8]{0:T(128)}, u32[]{:S(2)}) copy-start(f32[8]{0:T(128)} %bias_ref.1) | copy-start | bytes 100
  17.8 1.5 %collective-permute-start = (bf16[8,128,128]{2,1,0:T(8,128)(2,1)S(1)}, bf16[8,128,128]{2,1,0:T(8,128)(2,1)S(1)}, u32[]{:S(2)}, u32[]{:S(2)}) collective-permute-start(bf16[8,128,128]{2,1,0:T(8,128)(2,1)S(1)} %all_to_all.10.mine_ref.refs_0_), channel_id=1, source_target_pairs={{1,0},{0,1},{3,2},{2,3},{5,4},{4,5},{7,6},{6,7},{9,8},{8,9},{11,10... | collective-permute-start | bytes 786440 | tf_op jit(solution)/shard_map/ppermute | solution.py:331

commit v8 on v7

--- a/solution.py
+++ b/solution.py
@@ -48,9 +48,14 @@
     )(query, keys, values, grad_out)
 
 
+def owners(heads):
+    half = heads // 2
+    return [which * half + i for i in range(half) for which in range(2)]
+
+
 def frame_of(homes, shares, per_home, block, home, which):
     share = lax.rem(lax.axis_index("share") + block, shares)
-    return (home * shares + share) * per_home + which
+    return (owners(homes)[home] * shares + share) * per_home + which
 
 
 def query_weights(qg):
@@ -86,7 +91,9 @@
     slot = lax.broadcasted_iota(jnp.int32, (FRAME, PAIR), 0)
     lane = lax.broadcasted_iota(jnp.int32, (1, PAIR), 1)
 
-    bias = jnp.full((1, PAIR), bias_ref[lax.axis_index("heads")] / SCALE, jnp.float32)
+    me = lax.axis_index("heads")
+    head = sum(jnp.where(me == owner, i, 0) for i, owner in enumerate(owners(homes)))
+    bias = jnp.full((1, PAIR), bias_ref[head] / SCALE, jnp.float32)
     high = bias.astype(jnp.bfloat16).astype(jnp.float32)
     middle = (bias - high).astype(jnp.bfloat16).astype(jnp.float32)
     part = lax.rem(lane, 3)
@@ -323,7 +330,12 @@
 
 def local(query, keys, values, grad_out, valid, views, cross_bias):
     swap = functools.partial(
-        lax.all_to_all, axis_name="heads", split_axis=0, concat_axis=0, tiled=True
+        lax.all_to_all,
+        axis_name="heads",
+        split_axis=0,
+        concat_axis=0,
+        tiled=True,
+        axis_index_groups=[owners(lax.axis_size("heads"))],
     )
     shares = lax.axis_size("share")
     mine = swap(pack(query, keys, values, grad_out))

time: 34.7 us -> 34.8 us (level)
    all_to_all x1, blocking collectives: 16.1 us -> 16.6 us  [local(): mine = swap(pack(query, keys, values, grad_out))]
where the time goes in v8:
time: 34.8 us; the launch traced here: 34.6 us
  blocking collectives  28 us (80%)
  Pallas kernels  5.62 us (16%)
  between operations  0.69 us (2%)
    all_to_all x1, blocking collectives, local(): mine = swap(pack(query, keys, values, grad_out))  16.6 us
    all_to_all x1, blocking collectives, local(): return unpack(swap(given), query.shape[0])  11.4 us
    pallas_call x1, Pallas kernels, attend(): pl.pallas_call(functools.partial(finish_kernel, shares), out_shape=pltpu....  2.49 us
    pallas_call x1, Pallas kernels, attend(): pl.pallas_call(functools.partial(begin_kernel, shares), out_shape=(pltpu....  1.21 us
    pallas_call x1, Pallas kernels, pack(): pl.pallas_call(pack_kernel, out_shape=pltpu.VMEM((width // HD, 2 * rows,...  1.07 us
    pallas_call x1, Pallas kernels, unpack(): pl.pallas_call(unpack_kernel, out_shape=(shape,) * 3, in_specs=[VMEM], ou...  0.85 us
  transfers between devices with their start and end apart: 1, of which 1 were waited for; matrix products, arithmetic and copies ran while one was open for 0% of the time, Pallas kernels for 3%

profile of v8, /device:TPU:0, one launch (start us, length us, event | category | flops | bytes accessed | tf_op | source)
XLA Modules:
  0.0 34.6 jit_solution(8161518362460838870)
XLA Ops:
  0.6 1.1 %pack_heads.1 = bf16[8,128,128]{2,1,0:T(8,128)(2,1)S(1)} custom-call(bf16[64,512]{1,0:T(8,128)(2,1)} %q_ref.1, bf16[64,512]{1,0:T(8,128)(2,1)} %k_ref.1, bf16[64,512]{1,0:T(8,128)(2,1)} %v_ref.1, bf16[64,512]{1,0:T(8,128)(2,1)} %g_ref.1), custom_call_target="tpu_custom_call" | custom-call | tf_op jit(solution)/shard_map/pack_heads/pallas_call | solution.py:42
  1.7 0.0 copy-start
  1.7 0.0 copy-start.1
  1.7 0.0 copy-start.2
  1.7 16.6 %all_to_all.10.mine_ref.refs_0_ = bf16[8,128,128]{2,1,0:T(8,128)(2,1)S(1)} all-to-all(bf16[8,128,128]{2,1,0:T(8,128)(2,1)S(1)} %pack_heads.1), channel_id=1, replica_groups={{0,8,2,10,4,12,6,14},{1,9,3,11,5,13,7,15},{16,24,18,26,20,28,22,30},{17..., dimensions={0} | all-to-all | bytes 524288 | tf_op jit(solution)/shard_map/all_to_all | solution.py:341
  18.3 0.0 collective-permute-start
  18.3 0.0 copy-done
  18.3 0.0 copy-done.1
  18.4 0.0 copy-done.2
  18.4 1.2 %attend_begin.1 = (bf16[1024,128]{1,0:T(8,128)(2,1)S(1)}, bf16[1024,128]{1,0:T(8,128)(2,1)S(1)}, bf16[4,256,256]{2,1,0:T(8,128)(2,1)S(1)}, bf16[64,512]{1,0:T(8,...) custom-call(bf16[8,128,128]{2,1,0:T(8,128)(2,1)S(1)} %all_to_all.10.mine_ref, ...), custom_call_target="tpu_custom_call" | custom-call | flops 268435456 | bytes 2097152 | tf_op jit(solution)/shard_map/attend_begin/pallas_call | solution.py:269
  19.6 0.3 collective-permute-done.refs_1_
  19.9 2.5 %attend_finish.1 = bf16[8,96,128]{2,1,0:T(8,128)(2,1)S(1)} custom-call(bf16[8,128,128]{2,1,0:T(8,128)(2,1)S(1)} %all_to_all.10.mine_ref.refs_0_, bf16[8,128,128]{2,1,0:T(8,128)(2,1)S(1)} %collective-permute-done.refs_1_, bf16[1024,128]{1,0:T(8,128)(2,1)S(1)} %get-tuple-element.10.refs_2_, bf16[1024,128]{1,0:T(8,128)(2,1)S(1)} %get-tuple-element.11.refs_3_, ...), custom_call_target="tpu_custom_call" | custom-call | tf_op jit(solution)/shard_map/attend_finish/pallas_call | solution.py:289
  22.4 11.4 %all_to_all.11.in_ref = bf16[8,96,128]{2,1,0:T(8,128)(2,1)S(1)} all-to-all(bf16[8,96,128]{2,1,0:T(8,128)(2,1)S(1)} %attend_finish.1), channel_id=1, replica_groups={{0,8,2,10,4,12,6,14},{1,9,3,11,5,13,7,15},{16,24,18,26,20,28,22,30},{17..., dimensions={0} | all-to-all | bytes 393216 | tf_op jit(solution)/shard_map/all_to_all | solution.py:347
  33.7 0.9 %unpack_heads.1 = (f32[64,512]{1,0:T(8,128)}, f32[64,512]{1,0:T(8,128)}, f32[64,512]{1,0:T(8,128)}) custom-call(bf16[8,96,128]{2,1,0:T(8,128)(2,1)S(1)} %all_to_all.11.in_ref), custom_call_target="tpu_custom_call" | custom-call | tf_op jit(solution)/shard_map/unpack_heads/pallas_call | solution.py:322
Async XLA Ops:
  1.7 16.6 %copy-start = (s32[32]{0:T(128)S(1)}, s32[32]{0:T(128)}, u32[]{:S(2)}) copy-start(s32[32]{0:T(128)} %valid_ref.1) | copy-start | bytes 388
  1.7 16.6 %copy-start.1 = (s32[32]{0:T(128)S(1)}, s32[32]{0:T(128)}, u32[]{:S(2)}) copy-start(s32[32]{0:T(128)} %views_ref.1) | copy-start | bytes 388
  1.7 16.6 %copy-start.2 = (f32[8]{0:T(128)S(1)}, f32[8]{0:T(128)}, u32[]{:S(2)}) copy-start(f32[8]{0:T(128)} %bias_ref.1) | copy-start | bytes 100
  18.3 1.5 %collective-permute-start = (bf16[8,128,128]{2,1,0:T(8,128)(2,1)S(1)}, bf16[8,128,128]{2,1,0:T(8,128)(2,1)S(1)}, u32[]{:S(2)}, u32[]{:S(2)}) collective-permute-start(bf16[8,128,128]{2,1,0:T(8,128)(2,1)S(1)} %all_to_all.10.mine_ref.refs_0_), channel_id=1, source_target_pairs={{1,0},{0,1},{3,2},{2,3},{5,4},{4,5},{7,6},{6,7},{9,8},{8,9},{11,10... | collective-permute-start | bytes 786440 | tf_op jit(solution)/shard_map/ppermute | solution.py:343

commit v9 on v7

--- a/solution.py
+++ b/solution.py
@@ -57,7 +57,7 @@
     qg = qg.astype(jnp.float32)
     low = lax.broadcasted_iota(jnp.int32, qg.shape, 1) < HD
     return jnp.concatenate(
-        [jnp.where(low, qg, 0.0), jnp.where(low, 0.0, qg)], axis=0
+        [jnp.where(low, qg, 0.0), jnp.where(low, 0.0, qg * SCALE)], axis=0
     ).astype(jnp.bfloat16)
 
 
@@ -204,7 +204,7 @@
                     for ref in (expo_ref, gw_ref)
                 )
             weight = expo * (factors[c] * inverse)
-            grad = (weight * SCALE) * (gw - delta)
+            grad = weight * (gw - delta)
             grads.append(grad.reshape(CHUNK, TILE).astype(jnp.bfloat16))
             if c < own_chunks:
                 lows.append(weight.reshape(CHUNK, TILE).astype(jnp.bfloat16))
@@ -241,11 +241,13 @@
 
     others = tiles * (shares - 1)
     if shares <= 2:
-        pipeline([(True, i) for i in range(tiles)] + [(False, i) for i in range(others)])
+        pipeline([(False, i) for i in range(others)] + [(True, i) for i in range(tiles)])
     else:
         pl.loop(0, tiles, step=2)(lambda i: pipeline([(True, i), (True, i + 1)]))
         pl.loop(0, others, step=2)(lambda i: pipeline([(False, i), (False, i + 1)]))
-    out_ref[:, :rows, :] = sum_ref[...].astype(jnp.bfloat16).reshape(homes, rows, PAIR)
+    lane = lax.broadcasted_iota(jnp.int32, (1, PAIR), 1)
+    sums = sum_ref[...] * jnp.where(lane < HD, 1.0, 1.0 / SCALE)
+    out_ref[:, :rows, :] = sums.astype(jnp.bfloat16).reshape(homes, rows, PAIR)
     for home in range(homes):
         start, half = home * rows, rows // 2
         out_ref[home, rows:, :] = side_by_side(

time: 34.7 us -> 34.3 us (0.988)
  transfers between devices with their start and end apart: 1 -> 1, of which waited for: 1 -> 1; matrix products, arithmetic and copies ran while one was open for 0% -> 0% of each run, Pallas kernels for 3% -> 4%
where the time goes in v9:
time: 34.3 us; the launch traced here: 34.1 us
  blocking collectives  27.8 us (81%)
  Pallas kernels  5.29 us (15%)
  between operations  0.68 us (2%)
    all_to_all x1, blocking collectives, local(): mine = swap(pack(query, keys, values, grad_out))  16.1 us
    all_to_all x1, blocking collectives, local(): return unpack(swap(given), query.shape[0])  11.7 us
    pallas_call x1, Pallas kernels, attend(): pl.pallas_call(functools.partial(finish_kernel, shares), out_shape=pltpu....  2.17 us
    pallas_call x1, Pallas kernels, attend(): pl.pallas_call(functools.partial(begin_kernel, shares), out_shape=(pltpu....  1.19 us
    pallas_call x1, Pallas kernels, pack(): pl.pallas_call(pack_kernel, out_shape=pltpu.VMEM((width // HD, 2 * rows,...  1.07 us
    pallas_call x1, Pallas kernels, unpack(): pl.pallas_call(unpack_kernel, out_shape=(shape,) * 3, in_specs=[VMEM], ou...  0.85 us
  transfers between devices with their start and end apart: 1, of which 1 were waited for; matrix products, arithmetic and copies ran while one was open for 0% of the time, Pallas kernels for 4%

profile of v9, /device:TPU:0, one launch (start us, length us, event | category | flops | bytes accessed | tf_op | source)
XLA Modules:
  0.0 34.1 jit_solution(12611299109953840858)
XLA Ops:
  0.6 1.1 %pack_heads.1 = bf16[8,128,128]{2,1,0:T(8,128)(2,1)S(1)} custom-call(bf16[64,512]{1,0:T(8,128)(2,1)} %q_ref.1, bf16[64,512]{1,0:T(8,128)(2,1)} %k_ref.1, bf16[64,512]{1,0:T(8,128)(2,1)} %v_ref.1, bf16[64,512]{1,0:T(8,128)(2,1)} %g_ref.1), custom_call_target="tpu_custom_call" | custom-call | tf_op jit(solution)/shard_map/pack_heads/pallas_call | solution.py:42
  1.7 0.0 copy-start
  1.7 0.0 copy-start.1
  1.7 0.0 copy-start.2
  1.7 16.1 %all_to_all.10.mine_ref.refs_0_ = bf16[8,128,128]{2,1,0:T(8,128)(2,1)S(1)} all-to-all(bf16[8,128,128]{2,1,0:T(8,128)(2,1)S(1)} %pack_heads.1), channel_id=1, replica_groups=mesh['grp'=2,'blk'=4,'head'=4] {'blk','head':(1)2}, dimensions={0} | all-to-all | bytes 524288 | tf_op jit(solution)/shard_map/all_to_all | solution.py:331
  17.8 0.0 collective-permute-start
  17.8 0.0 copy-done
  17.8 0.0 copy-done.1
  17.9 0.0 copy-done.2
  17.9 1.2 %attend_begin.1 = (bf16[1024,128]{1,0:T(8,128)(2,1)S(1)}, bf16[1024,128]{1,0:T(8,128)(2,1)S(1)}, bf16[4,256,256]{2,1,0:T(8,128)(2,1)S(1)}, bf16[64,512]{1,0:T(8,...) custom-call(bf16[8,128,128]{2,1,0:T(8,128)(2,1)S(1)} %all_to_all.10.mine_ref, ...), custom_call_target="tpu_custom_call" | custom-call | flops 268435456 | bytes 2097152 | tf_op jit(solution)/shard_map/attend_begin/pallas_call | solution.py:264
  19.1 0.3 collective-permute-done.refs_1_
  19.4 2.2 %attend_finish.1 = bf16[8,96,128]{2,1,0:T(8,128)(2,1)S(1)} custom-call(bf16[8,128,128]{2,1,0:T(8,128)(2,1)S(1)} %all_to_all.10.mine_ref.refs_0_, bf16[8,128,128]{2,1,0:T(8,128)(2,1)S(1)} %collective-permute-done.refs_1_, bf16[1024,128]{1,0:T(8,128)(2,1)S(1)} %get-tuple-element.10.refs_2_, bf16[1024,128]{1,0:T(8,128)(2,1)S(1)} %get-tuple-element.11.refs_3_, ...), custom_call_target="tpu_custom_call" | custom-call | tf_op jit(solution)/shard_map/attend_finish/pallas_call | solution.py:284
  21.5 11.7 %all_to_all.11.in_ref = bf16[8,96,128]{2,1,0:T(8,128)(2,1)S(1)} all-to-all(bf16[8,96,128]{2,1,0:T(8,128)(2,1)S(1)} %attend_finish.1), channel_id=1, replica_groups=mesh['grp'=2,'blk'=4,'head'=4] {'blk','head':(1)2}, dimensions={0} | all-to-all | bytes 393216 | tf_op jit(solution)/shard_map/all_to_all | solution.py:337
  33.2 0.9 %unpack_heads.1 = (f32[64,512]{1,0:T(8,128)}, f32[64,512]{1,0:T(8,128)}, f32[64,512]{1,0:T(8,128)}) custom-call(bf16[8,96,128]{2,1,0:T(8,128)(2,1)S(1)} %all_to_all.11.in_ref), custom_call_target="tpu_custom_call" | custom-call | tf_op jit(solution)/shard_map/unpack_heads/pallas_call | solution.py:317
Async XLA Ops:
  1.7 16.1 %copy-start = (s32[32]{0:T(128)S(1)}, s32[32]{0:T(128)}, u32[]{:S(2)}) copy-start(s32[32]{0:T(128)} %valid_ref.1) | copy-start | bytes 388
  1.7 16.1 %copy-start.1 = (s32[32]{0:T(128)S(1)}, s32[32]{0:T(128)}, u32[]{:S(2)}) copy-start(s32[32]{0:T(128)} %views_ref.1) | copy-start | bytes 388
  1.7 16.1 %copy-start.2 = (f32[8]{0:T(128)S(1)}, f32[8]{0:T(128)}, u32[]{:S(2)}) copy-start(f32[8]{0:T(128)} %bias_ref.1) | copy-start | bytes 100
  17.8 1.5 %collective-permute-start = (bf16[8,128,128]{2,1,0:T(8,128)(2,1)S(1)}, bf16[8,128,128]{2,1,0:T(8,128)(2,1)S(1)}, u32[]{:S(2)}, u32[]{:S(2)}) collective-permute-start(bf16[8,128,128]{2,1,0:T(8,128)(2,1)S(1)} %all_to_all.10.mine_ref.refs_0_), channel_id=1, source_target_pairs={{1,0},{0,1},{3,2},{2,3},{5,4},{4,5},{7,6},{6,7},{9,8},{8,9},{11,10... | collective-permute-start | bytes 786440 | tf_op jit(solution)/shard_map/ppermute | solution.py:333

commit v10 on v9

--- a/solution.py
+++ b/solution.py
@@ -12,7 +12,7 @@
 FRAME = 32
 PAIR = 2 * HD
 TILE = 128
-CHUNK = 128
+CHUNK = 64
 SUBLANES = 8
 
 SCALE = 0.125

time: 34.3 us -> 34.3 us (level)
  transfers between devices with their start and end apart: 1 -> 1, of which waited for: 1 -> 1; matrix products, arithmetic and copies ran while one was open for 0% -> 0% of each run, Pallas kernels for 4% -> 3%
where the time goes in v10:
time: 34.3 us; the launch traced here: 34.1 us
  blocking collectives  27.8 us (81%)
  Pallas kernels  5.29 us (15%)
  between operations  0.68 us (2%)
    all_to_all x1, blocking collectives, local(): mine = swap(pack(query, keys, values, grad_out))  16.1 us
    all_to_all x1, blocking collectives, local(): return unpack(swap(given), query.shape[0])  11.7 us
    pallas_call x1, Pallas kernels, attend(): pl.pallas_call(functools.partial(finish_kernel, shares), out_shape=pltpu....  2.19 us
    pallas_call x1, Pallas kernels, attend(): pl.pallas_call(functools.partial(begin_kernel, shares), out_shape=(pltpu....  1.17 us
    pallas_call x1, Pallas kernels, pack(): pl.pallas_call(pack_kernel, out_shape=pltpu.VMEM((width // HD, 2 * rows,...  1.07 us
    pallas_call x1, Pallas kernels, unpack(): pl.pallas_call(unpack_kernel, out_shape=(shape,) * 3, in_specs=[VMEM], ou...  0.85 us
  transfers between devices with their start and end apart: 1, of which 1 were waited for; matrix products, arithmetic and copies ran while one was open for 0% of the time, Pallas kernels for 3%

profile of v10, /device:TPU:0, one launch (start us, length us, event | category | flops | bytes accessed | tf_op | source)
XLA Modules:
  0.0 34.1 jit_solution(450468416182545051)
XLA Ops:
  0.6 1.1 %pack_heads.1 = bf16[8,128,128]{2,1,0:T(8,128)(2,1)S(1)} custom-call(bf16[64,512]{1,0:T(8,128)(2,1)} %q_ref.1, bf16[64,512]{1,0:T(8,128)(2,1)} %k_ref.1, bf16[64,512]{1,0:T(8,128)(2,1)} %v_ref.1, bf16[64,512]{1,0:T(8,128)(2,1)} %g_ref.1), custom_call_target="tpu_custom_call" | custom-call | tf_op jit(solution)/shard_map/pack_heads/pallas_call | solution.py:42
  1.7 0.0 copy-start
  1.7 0.0 copy-start.1
  1.7 0.0 copy-start.2
  1.7 16.1 %all_to_all.10.mine_ref.refs_0_ = bf16[8,128,128]{2,1,0:T(8,128)(2,1)S(1)} all-to-all(bf16[8,128,128]{2,1,0:T(8,128)(2,1)S(1)} %pack_heads.1), channel_id=1, replica_groups=mesh['grp'=2,'blk'=4,'head'=4] {'blk','head':(1)2}, dimensions={0} | all-to-all | bytes 524288 | tf_op jit(solution)/shard_map/all_to_all | solution.py:331
  17.8 0.0 collective-permute-start
  17.8 0.0 copy-done
  17.8 0.0 copy-done.1
  17.9 0.0 copy-done.2
  17.9 1.2 %attend_begin.1 = (bf16[1024,128]{1,0:T(8,128)(2,1)S(1)}, bf16[1024,128]{1,0:T(8,128)(2,1)S(1)}, bf16[4,256,256]{2,1,0:T(8,128)(2,1)S(1)}, bf16[64,512]{1,0:T(8,...) custom-call(bf16[8,128,128]{2,1,0:T(8,128)(2,1)S(1)} %all_to_all.10.mine_ref, ...), custom_call_target="tpu_custom_call" | custom-call | flops 268435456 | bytes 2097152 | tf_op jit(solution)/shard_map/attend_begin/pallas_call | solution.py:264
  19.0 0.3 collective-permute-done.refs_1_
  19.4 2.2 %attend_finish.1 = bf16[8,96,128]{2,1,0:T(8,128)(2,1)S(1)} custom-call(bf16[8,128,128]{2,1,0:T(8,128)(2,1)S(1)} %all_to_all.10.mine_ref.refs_0_, bf16[8,128,128]{2,1,0:T(8,128)(2,1)S(1)} %collective-permute-done.refs_1_, bf16[1024,128]{1,0:T(8,128)(2,1)S(1)} %get-tuple-element.10.refs_2_, bf16[1024,128]{1,0:T(8,128)(2,1)S(1)} %get-tuple-element.11.refs_3_, ...), custom_call_target="tpu_custom_call" | custom-call | tf_op jit(solution)/shard_map/attend_finish/pallas_call | solution.py:284
  21.6 11.7 %all_to_all.11.in_ref = bf16[8,96,128]{2,1,0:T(8,128)(2,1)S(1)} all-to-all(bf16[8,96,128]{2,1,0:T(8,128)(2,1)S(1)} %attend_finish.1), channel_id=1, replica_groups=mesh['grp'=2,'blk'=4,'head'=4] {'blk','head':(1)2}, dimensions={0} | all-to-all | bytes 393216 | tf_op jit(solution)/shard_map/all_to_all | solution.py:337
  33.2 0.9 %unpack_heads.1 = (f32[64,512]{1,0:T(8,128)}, f32[64,512]{1,0:T(8,128)}, f32[64,512]{1,0:T(8,128)}) custom-call(bf16[8,96,128]{2,1,0:T(8,128)(2,1)S(1)} %all_to_all.11.in_ref), custom_call_target="tpu_custom_call" | custom-call | tf_op jit(solution)/shard_map/unpack_heads/pallas_call | solution.py:317
Async XLA Ops:
  1.7 16.1 %copy-start = (s32[32]{0:T(128)S(1)}, s32[32]{0:T(128)}, u32[]{:S(2)}) copy-start(s32[32]{0:T(128)} %valid_ref.1) | copy-start | bytes 388
  1.7 16.1 %copy-start.1 = (s32[32]{0:T(128)S(1)}, s32[32]{0:T(128)}, u32[]{:S(2)}) copy-start(s32[32]{0:T(128)} %views_ref.1) | copy-start | bytes 388
  1.7 16.1 %copy-start.2 = (f32[8]{0:T(128)S(1)}, f32[8]{0:T(128)}, u32[]{:S(2)}) copy-start(f32[8]{0:T(128)} %bias_ref.1) | copy-start | bytes 100
  17.8 1.5 %collective-permute-start = (bf16[8,128,128]{2,1,0:T(8,128)(2,1)S(1)}, bf16[8,128,128]{2,1,0:T(8,128)(2,1)S(1)}, u32[]{:S(2)}, u32[]{:S(2)}) collective-permute-start(bf16[8,128,128]{2,1,0:T(8,128)(2,1)S(1)} %all_to_all.10.mine_ref.refs_0_), channel_id=1, source_target_pairs={{1,0},{0,1},{3,2},{2,3},{5,4},{4,5},{7,6},{6,7},{9,8},{8,9},{11,10... | collective-permute-start | bytes 786440 | tf_op jit(solution)/shard_map/ppermute | solution.py:333

commit v11 on v9

--- a/solution.py
+++ b/solution.py
@@ -227,17 +227,17 @@
 
     def pipeline(work):
         scored, expos, done = {}, {}, {}
-        for step in range(len(work) + 2):
+        for step in range(len(work) + 3):
             if step < len(work):
                 scored[step] = score(*work[step])
+            if 4 <= step and step % 2 == 0:
+                leave(*work[step - 4], (done.pop(step - 4), done.pop(step - 3)))
             if 0 <= step - 1 < len(work):
                 weights, both = scored.pop(step - 1)
                 expos[step - 1] = weights, all_exponentials(*work[step - 1], both)
-            if 0 <= step - 2:
+            if 0 <= step - 2 < len(work):
                 weights, parts = expos.pop(step - 2)
                 done[step - 2] = (weights, *gradients(*work[step - 2], parts))
-                if step % 2:
-                    leave(*work[step - 3], (done.pop(step - 3), done.pop(step - 2)))
 
     others = tiles * (shares - 1)
     if shares <= 2:

time: 34.3 us -> 34.4 us (level)
  transfers between devices with their start and end apart: 1 -> 1, of which waited for: 1 -> 1; matrix products, arithmetic and copies ran while one was open for 0% -> 0% of each run, Pallas kernels for 4% -> 3%
where the time goes in v11:
time: 34.4 us; the launch traced here: 34.2 us
  blocking collectives  27.8 us (81%)
  Pallas kernels  5.34 us (16%)
  between operations  0.68 us (2%)
    all_to_all x1, blocking collectives, local(): mine = swap(pack(query, keys, values, grad_out))  16.1 us
    all_to_all x1, blocking collectives, local(): return unpack(swap(given), query.shape[0])  11.7 us
    pallas_call x1, Pallas kernels, attend(): pl.pallas_call(functools.partial(finish_kernel, shares), out_shape=pltpu....  2.23 us
    pallas_call x1, Pallas kernels, attend(): pl.pallas_call(functools.partial(begin_kernel, shares), out_shape=(pltpu....  1.19 us
    pallas_call x1, Pallas kernels, pack(): pl.pallas_call(pack_kernel, out_shape=pltpu.VMEM((width // HD, 2 * rows,...  1.07 us
    pallas_call x1, Pallas kernels, unpack(): pl.pallas_call(unpack_kernel, out_shape=(shape,) * 3, in_specs=[VMEM], ou...  0.85 us
  transfers between devices with their start and end apart: 1, of which 1 were waited for; matrix products, arithmetic and copies ran while one was open for 0% of the time, Pallas kernels for 3%

profile of v11, /device:TPU:0, one launch (start us, length us, event | category | flops | bytes accessed | tf_op | source)
XLA Modules:
  0.0 34.2 jit_solution(18126057281782051861)
XLA Ops:
  0.6 1.1 %pack_heads.1 = bf16[8,128,128]{2,1,0:T(8,128)(2,1)S(1)} custom-call(bf16[64,512]{1,0:T(8,128)(2,1)} %q_ref.1, bf16[64,512]{1,0:T(8,128)(2,1)} %k_ref.1, bf16[64,512]{1,0:T(8,128)(2,1)} %v_ref.1, bf16[64,512]{1,0:T(8,128)(2,1)} %g_ref.1), custom_call_target="tpu_custom_call" | custom-call | tf_op jit(solution)/shard_map/pack_heads/pallas_call | solution.py:42
  1.7 0.0 copy-start
  1.7 0.0 copy-start.1
  1.7 0.0 copy-start.2
  1.7 16.1 %all_to_all.10.mine_ref.refs_0_ = bf16[8,128,128]{2,1,0:T(8,128)(2,1)S(1)} all-to-all(bf16[8,128,128]{2,1,0:T(8,128)(2,1)S(1)} %pack_heads.1), channel_id=1, replica_groups=mesh['grp'=2,'blk'=4,'head'=4] {'blk','head':(1)2}, dimensions={0} | all-to-all | bytes 524288 | tf_op jit(solution)/shard_map/all_to_all | solution.py:331
  17.8 0.0 collective-permute-start
  17.8 0.0 copy-done
  17.8 0.0 copy-done.1
  17.9 0.0 copy-done.2
  17.9 1.2 %attend_begin.1 = (bf16[1024,128]{1,0:T(8,128)(2,1)S(1)}, bf16[1024,128]{1,0:T(8,128)(2,1)S(1)}, bf16[4,256,256]{2,1,0:T(8,128)(2,1)S(1)}, bf16[64,512]{1,0:T(8,...) custom-call(bf16[8,128,128]{2,1,0:T(8,128)(2,1)S(1)} %all_to_all.10.mine_ref, ...), custom_call_target="tpu_custom_call" | custom-call | flops 268435456 | bytes 2097152 | tf_op jit(solution)/shard_map/attend_begin/pallas_call | solution.py:264
  19.1 0.3 collective-permute-done.refs_1_
  19.4 2.2 %attend_finish.1 = bf16[8,96,128]{2,1,0:T(8,128)(2,1)S(1)} custom-call(bf16[8,128,128]{2,1,0:T(8,128)(2,1)S(1)} %all_to_all.10.mine_ref.refs_0_, bf16[8,128,128]{2,1,0:T(8,128)(2,1)S(1)} %collective-permute-done.refs_1_, bf16[1024,128]{1,0:T(8,128)(2,1)S(1)} %get-tuple-element.10.refs_2_, bf16[1024,128]{1,0:T(8,128)(2,1)S(1)} %get-tuple-element.11.refs_3_, ...), custom_call_target="tpu_custom_call" | custom-call | tf_op jit(solution)/shard_map/attend_finish/pallas_call | solution.py:284
  21.6 11.7 %all_to_all.11.in_ref = bf16[8,96,128]{2,1,0:T(8,128)(2,1)S(1)} all-to-all(bf16[8,96,128]{2,1,0:T(8,128)(2,1)S(1)} %attend_finish.1), channel_id=1, replica_groups=mesh['grp'=2,'blk'=4,'head'=4] {'blk','head':(1)2}, dimensions={0} | all-to-all | bytes 393216 | tf_op jit(solution)/shard_map/all_to_all | solution.py:337
  33.3 0.9 %unpack_heads.1 = (f32[64,512]{1,0:T(8,128)}, f32[64,512]{1,0:T(8,128)}, f32[64,512]{1,0:T(8,128)}) custom-call(bf16[8,96,128]{2,1,0:T(8,128)(2,1)S(1)} %all_to_all.11.in_ref), custom_call_target="tpu_custom_call" | custom-call | tf_op jit(solution)/shard_map/unpack_heads/pallas_call | solution.py:317
Async XLA Ops:
  1.7 16.1 %copy-start = (s32[32]{0:T(128)S(1)}, s32[32]{0:T(128)}, u32[]{:S(2)}) copy-start(s32[32]{0:T(128)} %valid_ref.1) | copy-start | bytes 388
  1.7 16.1 %copy-start.1 = (s32[32]{0:T(128)S(1)}, s32[32]{0:T(128)}, u32[]{:S(2)}) copy-start(s32[32]{0:T(128)} %views_ref.1) | copy-start | bytes 388
  1.7 16.1 %copy-start.2 = (f32[8]{0:T(128)S(1)}, f32[8]{0:T(128)}, u32[]{:S(2)}) copy-start(f32[8]{0:T(128)} %bias_ref.1) | copy-start | bytes 100
  17.8 1.5 %collective-permute-start = (bf16[8,128,128]{2,1,0:T(8,128)(2,1)S(1)}, bf16[8,128,128]{2,1,0:T(8,128)(2,1)S(1)}, u32[]{:S(2)}, u32[]{:S(2)}) collective-permute-start(bf16[8,128,128]{2,1,0:T(8,128)(2,1)S(1)} %all_to_all.10.mine_ref.refs_0_), channel_id=1, source_target_pairs={{1,0},{0,1},{3,2},{2,3},{5,4},{4,5},{7,6},{6,7},{9,8},{8,9},{11,10... | collective-permute-start | bytes 786440 | tf_op jit(solution)/shard_map/ppermute | solution.py:333

commit v12 on v9

--- a/solution.py
+++ b/solution.py
@@ -241,7 +241,10 @@
 
     others = tiles * (shares - 1)
     if shares <= 2:
-        pipeline([(False, i) for i in range(others)] + [(True, i) for i in range(tiles)])
+        work = [[(False, i), (False, i + 1)] for i in range(0, others, 2)]
+        mine = [[(True, i), (True, i + 1)] for i in range(0, tiles, 2)]
+        turns = [pair for both in zip(work, mine) for pair in both] if work else mine
+        pipeline([tile for pair in turns for tile in pair])
     else:
         pl.loop(0, tiles, step=2)(lambda i: pipeline([(True, i), (True, i + 1)]))
         pl.loop(0, others, step=2)(lambda i: pipeline([(False, i), (False, i + 1)]))

time: 34.3 us -> 34.7 us (1.012)
  Pallas kernels: 5.29 us -> 5.68 us
    pallas_call x1, Pallas kernels: 2.17 us -> 2.56 us  [attend(): pl.pallas_call(functools.partial(finish_kernel, shares), out_shape=pltpu....]
  transfers between devices with their start and end apart: 1 -> 1, of which waited for: 1 -> 1; matrix products, arithmetic and copies ran while one was open for 0% -> 0% of each run, Pallas kernels for 4% -> 3%
where the time goes in v12:
time: 34.7 us; the launch traced here: 34.5 us
  blocking collectives  27.8 us (80%)
  Pallas kernels  5.68 us (16%)
  between operations  0.68 us (2%)
    all_to_all x1, blocking collectives, local(): mine = swap(pack(query, keys, values, grad_out))  16.1 us
    all_to_all x1, blocking collectives, local(): return unpack(swap(given), query.shape[0])  11.7 us
    pallas_call x1, Pallas kernels, attend(): pl.pallas_call(functools.partial(finish_kernel, shares), out_shape=pltpu....  2.56 us
    pallas_call x1, Pallas kernels, attend(): pl.pallas_call(functools.partial(begin_kernel, shares), out_shape=(pltpu....  1.19 us
    pallas_call x1, Pallas kernels, pack(): pl.pallas_call(pack_kernel, out_shape=pltpu.VMEM((width // HD, 2 * rows,...  1.07 us
    pallas_call x1, Pallas kernels, unpack(): pl.pallas_call(unpack_kernel, out_shape=(shape,) * 3, in_specs=[VMEM], ou...  0.85 us
  transfers between devices with their start and end apart: 1, of which 1 were waited for; matrix products, arithmetic and copies ran while one was open for 0% of the time, Pallas kernels for 3%

profile of v12, /device:TPU:0, one launch (start us, length us, event | category | flops | bytes accessed | tf_op | source)
XLA Modules:
  0.0 34.5 jit_solution(8952916905334972527)
XLA Ops:
  0.6 1.1 %pack_heads.1 = bf16[8,128,128]{2,1,0:T(8,128)(2,1)S(1)} custom-call(bf16[64,512]{1,0:T(8,128)(2,1)} %q_ref.1, bf16[64,512]{1,0:T(8,128)(2,1)} %k_ref.1, bf16[64,512]{1,0:T(8,128)(2,1)} %v_ref.1, bf16[64,512]{1,0:T(8,128)(2,1)} %g_ref.1), custom_call_target="tpu_custom_call" | custom-call | tf_op jit(solution)/shard_map/pack_heads/pallas_call | solution.py:42
  1.7 0.0 copy-start
  1.7 0.0 copy-start.1
  1.7 0.0 copy-start.2
  1.7 16.1 %all_to_all.10.mine_ref.refs_0_ = bf16[8,128,128]{2,1,0:T(8,128)(2,1)S(1)} all-to-all(bf16[8,128,128]{2,1,0:T(8,128)(2,1)S(1)} %pack_heads.1), channel_id=1, replica_groups=mesh['grp'=2,'blk'=4,'head'=4] {'blk','head':(1)2}, dimensions={0} | all-to-all | bytes 524288 | tf_op jit(solution)/shard_map/all_to_all | solution.py:334
  17.8 0.0 collective-permute-start
  17.8 0.0 copy-done
  17.8 0.0 copy-done.1
  17.9 0.0 copy-done.2
  17.9 1.2 %attend_begin.1 = (bf16[1024,128]{1,0:T(8,128)(2,1)S(1)}, bf16[1024,128]{1,0:T(8,128)(2,1)S(1)}, bf16[4,256,256]{2,1,0:T(8,128)(2,1)S(1)}, bf16[64,512]{1,0:T(8,...) custom-call(bf16[8,128,128]{2,1,0:T(8,128)(2,1)S(1)} %all_to_all.10.mine_ref, ...), custom_call_target="tpu_custom_call" | custom-call | flops 268435456 | bytes 2097152 | tf_op jit(solution)/shard_map/attend_begin/pallas_call | solution.py:267
  19.1 0.3 collective-permute-done.refs_1_
  19.4 2.6 %attend_finish.1 = bf16[8,96,128]{2,1,0:T(8,128)(2,1)S(1)} custom-call(bf16[8,128,128]{2,1,0:T(8,128)(2,1)S(1)} %all_to_all.10.mine_ref.refs_0_, bf16[8,128,128]{2,1,0:T(8,128)(2,1)S(1)} %collective-permute-done.refs_1_, bf16[1024,128]{1,0:T(8,128)(2,1)S(1)} %get-tuple-element.10.refs_2_, bf16[1024,128]{1,0:T(8,128)(2,1)S(1)} %get-tuple-element.11.refs_3_, ...), custom_call_target="tpu_custom_call" | custom-call | tf_op jit(solution)/shard_map/attend_finish/pallas_call | solution.py:287
  21.9 11.7 %all_to_all.11.in_ref = bf16[8,96,128]{2,1,0:T(8,128)(2,1)S(1)} all-to-all(bf16[8,96,128]{2,1,0:T(8,128)(2,1)S(1)} %attend_finish.1), channel_id=1, replica_groups=mesh['grp'=2,'blk'=4,'head'=4] {'blk','head':(1)2}, dimensions={0} | all-to-all | bytes 393216 | tf_op jit(solution)/shard_map/all_to_all | solution.py:340
  33.6 0.9 %unpack_heads.1 = (f32[64,512]{1,0:T(8,128)}, f32[64,512]{1,0:T(8,128)}, f32[64,512]{1,0:T(8,128)}) custom-call(bf16[8,96,128]{2,1,0:T(8,128)(2,1)S(1)} %all_to_all.11.in_ref), custom_call_target="tpu_custom_call" | custom-call | tf_op jit(solution)/shard_map/unpack_heads/pallas_call | solution.py:320
Async XLA Ops:
  1.7 16.1 %copy-start = (s32[32]{0:T(128)S(1)}, s32[32]{0:T(128)}, u32[]{:S(2)}) copy-start(s32[32]{0:T(128)} %valid_ref.1) | copy-start | bytes 388
  1.7 16.1 %copy-start.1 = (s32[32]{0:T(128)S(1)}, s32[32]{0:T(128)}, u32[]{:S(2)}) copy-start(s32[32]{0:T(128)} %views_ref.1) | copy-start | bytes 388
  1.7 16.1 %copy-start.2 = (f32[8]{0:T(128)S(1)}, f32[8]{0:T(128)}, u32[]{:S(2)}) copy-start(f32[8]{0:T(128)} %bias_ref.1) | copy-start | bytes 100
  17.8 1.5 %collective-permute-start = (bf16[8,128,128]{2,1,0:T(8,128)(2,1)S(1)}, bf16[8,128,128]{2,1,0:T(8,128)(2,1)S(1)}, u32[]{:S(2)}, u32[]{:S(2)}) collective-permute-start(bf16[8,128,128]{2,1,0:T(8,128)(2,1)S(1)} %all_to_all.10.mine_ref.refs_0_), channel_id=1, source_target_pairs={{1,0},{0,1},{3,2},{2,3},{5,4},{4,5},{7,6},{6,7},{9,8},{8,9},{11,10... | collective-permute-start | bytes 786440 | tf_op jit(solution)/shard_map/ppermute | solution.py:336

commit v13 on v9

--- a/solution.py
+++ b/solution.py
@@ -210,8 +210,8 @@
                 lows.append(weight.reshape(CHUNK, TILE).astype(jnp.bfloat16))
         return jnp.concatenate(grads, axis=0), jnp.concatenate(lows, axis=0)
 
-    def leave(ours, first, pair):
-        weights, grads, lows = zip(*pair)
+    def leave(ours, first, group):
+        weights, grads, lows = zip(*group)
         factors = [x for both in zip(grads, lows) for x in (both[0][:own], both[1])]
         sum_ref[...] += jnp.dot(
             jnp.concatenate(factors, axis=1),
@@ -225,8 +225,9 @@
             here = pl.ds(pl.multiple_of(first * TILE, 2 * TILE), 2 * TILE)
             dq_ref[here, :] = jnp.concatenate([turned, turned], axis=0).T
 
-    def pipeline(work):
-        scored, expos, done = {}, {}, {}
+    def pipeline(groups):
+        work = [tile for group in groups for tile in group]
+        scored, expos, done, groups = {}, {}, [], list(groups)
         for step in range(len(work) + 2):
             if step < len(work):
                 scored[step] = score(*work[step])
@@ -235,16 +236,18 @@
                 expos[step - 1] = weights, all_exponentials(*work[step - 1], both)
             if 0 <= step - 2:
                 weights, parts = expos.pop(step - 2)
-                done[step - 2] = (weights, *gradients(*work[step - 2], parts))
-                if step % 2:
-                    leave(*work[step - 3], (done.pop(step - 3), done.pop(step - 2)))
+                done.append((weights, *gradients(*work[step - 2], parts)))
+                if len(done) == len(groups[0]):
+                    leave(*groups.pop(0)[0], done)
+                    done = []
 
     others = tiles * (shares - 1)
     if shares <= 2:
-        pipeline([(False, i) for i in range(others)] + [(True, i) for i in range(tiles)])
+        theirs = [[(False, i) for i in range(others)]] if others else []
+        pipeline(theirs + [[(True, i), (True, i + 1)] for i in range(0, tiles, 2)])
     else:
-        pl.loop(0, tiles, step=2)(lambda i: pipeline([(True, i), (True, i + 1)]))
-        pl.loop(0, others, step=2)(lambda i: pipeline([(False, i), (False, i + 1)]))
+        pl.loop(0, tiles, step=2)(lambda i: pipeline([[(True, i), (True, i + 1)]]))
+        pl.loop(0, others, step=2)(lambda i: pipeline([[(False, i), (False, i + 1)]]))
     lane = lax.broadcasted_iota(jnp.int32, (1, PAIR), 1)
     sums = sum_ref[...] * jnp.where(lane < HD, 1.0, 1.0 / SCALE)
     out_ref[:, :rows, :] = sums.astype(jnp.bfloat16).reshape(homes, rows, PAIR)

time: 34.3 us -> 34.4 us (level)
  no operation moved by 1% of the time
where the time goes in v13:
time: 34.4 us; the launch traced here: 34.1 us
  blocking collectives  27.8 us (81%)
  Pallas kernels  5.32 us (15%)
  between operations  0.68 us (2%)
    all_to_all x1, blocking collectives, local(): mine = swap(pack(query, keys, values, grad_out))  16.1 us
    all_to_all x1, blocking collectives, local(): return unpack(swap(given), query.shape[0])  11.7 us
    pallas_call x1, Pallas kernels, attend(): pl.pallas_call(functools.partial(finish_kernel, shares), out_shape=pltpu....  2.2 us
    pallas_call x1, Pallas kernels, attend(): pl.pallas_call(functools.partial(begin_kernel, shares), out_shape=(pltpu....  1.19 us
    pallas_call x1, Pallas kernels, pack(): pl.pallas_call(pack_kernel, out_shape=pltpu.VMEM((width // HD, 2 * rows,...  1.07 us
    pallas_call x1, Pallas kernels, unpack(): pl.pallas_call(unpack_kernel, out_shape=(shape,) * 3, in_specs=[VMEM], ou...  0.85 us
  transfers between devices with their start and end apart: 1, of which 1 were waited for; matrix products, arithmetic and copies ran while one was open for 0% of the time, Pallas kernels for 4%

profile of v13, /device:TPU:0, one launch (start us, length us, event | category | flops | bytes accessed | tf_op | source)
XLA Modules:
  0.0 34.1 jit_solution(14595839775605659698)
XLA Ops:
  0.6 1.1 %pack_heads.1 = bf16[8,128,128]{2,1,0:T(8,128)(2,1)S(1)} custom-call(bf16[64,512]{1,0:T(8,128)(2,1)} %q_ref.1, bf16[64,512]{1,0:T(8,128)(2,1)} %k_ref.1, bf16[64,512]{1,0:T(8,128)(2,1)} %v_ref.1, bf16[64,512]{1,0:T(8,128)(2,1)} %g_ref.1), custom_call_target="tpu_custom_call" | custom-call | tf_op jit(solution)/shard_map/pack_heads/pallas_call | solution.py:42
  1.7 0.0 copy-start
  1.7 0.0 copy-start.1
  1.7 0.0 copy-start.2
  1.7 16.1 %all_to_all.10.mine_ref.refs_0_ = bf16[8,128,128]{2,1,0:T(8,128)(2,1)S(1)} all-to-all(bf16[8,128,128]{2,1,0:T(8,128)(2,1)S(1)} %pack_heads.1), channel_id=1, replica_groups=mesh['grp'=2,'blk'=4,'head'=4] {'blk','head':(1)2}, dimensions={0} | all-to-all | bytes 524288 | tf_op jit(solution)/shard_map/all_to_all | solution.py:334
  17.8 0.0 collective-permute-start
  17.8 0.0 copy-done
  17.8 0.0 copy-done.1
  17.9 0.0 copy-done.2
  17.9 1.2 %attend_begin.1 = (bf16[1024,128]{1,0:T(8,128)(2,1)S(1)}, bf16[1024,128]{1,0:T(8,128)(2,1)S(1)}, bf16[4,256,256]{2,1,0:T(8,128)(2,1)S(1)}, bf16[64,512]{1,0:T(8,...) custom-call(bf16[8,128,128]{2,1,0:T(8,128)(2,1)S(1)} %all_to_all.10.mine_ref, ...), custom_call_target="tpu_custom_call" | custom-call | flops 268435456 | bytes 2097152 | tf_op jit(solution)/shard_map/attend_begin/pallas_call | solution.py:267
  19.1 0.3 collective-permute-done.refs_1_
  19.4 2.2 %attend_finish.1 = bf16[8,96,128]{2,1,0:T(8,128)(2,1)S(1)} custom-call(bf16[8,128,128]{2,1,0:T(8,128)(2,1)S(1)} %all_to_all.10.mine_ref.refs_0_, bf16[8,128,128]{2,1,0:T(8,128)(2,1)S(1)} %collective-permute-done.refs_1_, bf16[1024,128]{1,0:T(8,128)(2,1)S(1)} %get-tuple-element.10.refs_2_, bf16[1024,128]{1,0:T(8,128)(2,1)S(1)} %get-tuple-element.11.refs_3_, ...), custom_call_target="tpu_custom_call" | custom-call | tf_op jit(solution)/shard_map/attend_finish/pallas_call | solution.py:287
  21.6 11.7 %all_to_all.11.in_ref = bf16[8,96,128]{2,1,0:T(8,128)(2,1)S(1)} all-to-all(bf16[8,96,128]{2,1,0:T(8,128)(2,1)S(1)} %attend_finish.1), channel_id=1, replica_groups=mesh['grp'=2,'blk'=4,'head'=4] {'blk','head':(1)2}, dimensions={0} | all-to-all | bytes 393216 | tf_op jit(solution)/shard_map/all_to_all | solution.py:340
  33.3 0.9 %unpack_heads.1 = (f32[64,512]{1,0:T(8,128)}, f32[64,512]{1,0:T(8,128)}, f32[64,512]{1,0:T(8,128)}) custom-call(bf16[8,96,128]{2,1,0:T(8,128)(2,1)S(1)} %all_to_all.11.in_ref), custom_call_target="tpu_custom_call" | custom-call | tf_op jit(solution)/shard_map/unpack_heads/pallas_call | solution.py:320
Async XLA Ops:
  1.7 16.1 %copy-start = (s32[32]{0:T(128)S(1)}, s32[32]{0:T(128)}, u32[]{:S(2)}) copy-start(s32[32]{0:T(128)} %valid_ref.1) | copy-start | bytes 388
  1.7 16.1 %copy-start.1 = (s32[32]{0:T(128)S(1)}, s32[32]{0:T(128)}, u32[]{:S(2)}) copy-start(s32[32]{0:T(128)} %views_ref.1) | copy-start | bytes 388
  1.7 16.1 %copy-start.2 = (f32[8]{0:T(128)S(1)}, f32[8]{0:T(128)}, u32[]{:S(2)}) copy-start(f32[8]{0:T(128)} %bias_ref.1) | copy-start | bytes 100
  17.8 1.5 %collective-permute-start = (bf16[8,128,128]{2,1,0:T(8,128)(2,1)S(1)}, bf16[8,128,128]{2,1,0:T(8,128)(2,1)S(1)}, u32[]{:S(2)}, u32[]{:S(2)}) collective-permute-start(bf16[8,128,128]{2,1,0:T(8,128)(2,1)S(1)} %all_to_all.10.mine_ref.refs_0_), channel_id=1, source_target_pairs={{1,0},{0,1},{3,2},{2,3},{5,4},{4,5},{7,6},{6,7},{9,8},{8,9},{11,10... | collective-permute-start | bytes 786440 | tf_op jit(solution)/shard_map/ppermute | solution.py:336

commit v14 on v10

--- a/solution.py
+++ b/solution.py
@@ -12,7 +12,7 @@
 FRAME = 32
 PAIR = 2 * HD
 TILE = 128
-CHUNK = 64
+CHUNK = 256
 SUBLANES = 8
 
 SCALE = 0.125

time: 34.3 us -> 34.6 us (level)
  transfers between devices with their start and end apart: 1 -> 1, of which waited for: 1 -> 1; matrix products, arithmetic and copies ran while one was open for 0% -> 0% of each run, Pallas kernels for 3% -> 4%
where the time goes in v14:
time: 34.6 us; the launch traced here: 34.3 us
  blocking collectives  27.9 us (81%)
  Pallas kernels  5.51 us (16%)
  between operations  0.68 us (2%)
    all_to_all x1, blocking collectives, local(): mine = swap(pack(query, keys, values, grad_out))  16.1 us
    all_to_all x1, blocking collectives, local(): return unpack(swap(given), query.shape[0])  11.8 us
    pallas_call x1, Pallas kernels, attend(): pl.pallas_call(functools.partial(finish_kernel, shares), out_shape=pltpu....  2.32 us
    pallas_call x1, Pallas kernels, attend(): pl.pallas_call(functools.partial(begin_kernel, shares), out_shape=(pltpu....  1.27 us
    pallas_call x1, Pallas kernels, pack(): pl.pallas_call(pack_kernel, out_shape=pltpu.VMEM((width // HD, 2 * rows,...  1.07 us
    pallas_call x1, Pallas kernels, unpack(): pl.pallas_call(unpack_kernel, out_shape=(shape,) * 3, in_specs=[VMEM], ou...  0.85 us
  transfers between devices with their start and end apart: 1, of which 1 were waited for; matrix products, arithmetic and copies ran while one was open for 0% of the time, Pallas kernels for 4%

profile of v14, /device:TPU:0, one launch (start us, length us, event | category | flops | bytes accessed | tf_op | source)
XLA Modules:
  0.0 34.3 jit_solution(6077811652512381164)
XLA Ops:
  0.6 1.1 %pack_heads.1 = bf16[8,128,128]{2,1,0:T(8,128)(2,1)S(1)} custom-call(bf16[64,512]{1,0:T(8,128)(2,1)} %q_ref.1, bf16[64,512]{1,0:T(8,128)(2,1)} %k_ref.1, bf16[64,512]{1,0:T(8,128)(2,1)} %v_ref.1, bf16[64,512]{1,0:T(8,128)(2,1)} %g_ref.1), custom_call_target="tpu_custom_call" | custom-call | tf_op jit(solution)/shard_map/pack_heads/pallas_call | solution.py:42
  1.7 0.0 copy-start
  1.7 0.0 copy-start.1
  1.7 0.0 copy-start.2
  1.7 16.1 %all_to_all.10.mine_ref.refs_0_ = bf16[8,128,128]{2,1,0:T(8,128)(2,1)S(1)} all-to-all(bf16[8,128,128]{2,1,0:T(8,128)(2,1)S(1)} %pack_heads.1), channel_id=1, replica_groups=mesh['grp'=2,'blk'=4,'head'=4] {'blk','head':(1)2}, dimensions={0} | all-to-all | bytes 524288 | tf_op jit(solution)/shard_map/all_to_all | solution.py:331
  17.8 0.0 collective-permute-start
  17.8 0.0 copy-done
  17.8 0.0 copy-done.1
  17.9 0.0 copy-done.2
  17.9 1.3 %attend_begin.1 = (bf16[1024,128]{1,0:T(8,128)(2,1)S(1)}, bf16[1024,128]{1,0:T(8,128)(2,1)S(1)}, bf16[4,256,256]{2,1,0:T(8,128)(2,1)S(1)}, bf16[64,512]{1,0:T(8,...) custom-call(bf16[8,128,128]{2,1,0:T(8,128)(2,1)S(1)} %all_to_all.10.mine_ref, ...), custom_call_target="tpu_custom_call" | custom-call | flops 268435456 | bytes 2097152 | tf_op jit(solution)/shard_map/attend_begin/pallas_call | solution.py:264
  19.1 0.2 collective-permute-done.refs_1_
  19.4 2.3 %attend_finish.1 = bf16[8,96,128]{2,1,0:T(8,128)(2,1)S(1)} custom-call(bf16[8,128,128]{2,1,0:T(8,128)(2,1)S(1)} %all_to_all.10.mine_ref.refs_0_, bf16[8,128,128]{2,1,0:T(8,128)(2,1)S(1)} %collective-permute-done.refs_1_, bf16[1024,128]{1,0:T(8,128)(2,1)S(1)} %get-tuple-element.10.refs_2_, bf16[1024,128]{1,0:T(8,128)(2,1)S(1)} %get-tuple-element.11.refs_3_, ...), custom_call_target="tpu_custom_call" | custom-call | tf_op jit(solution)/shard_map/attend_finish/pallas_call | solution.py:284
  21.7 11.8 %all_to_all.11.in_ref = bf16[8,96,128]{2,1,0:T(8,128)(2,1)S(1)} all-to-all(bf16[8,96,128]{2,1,0:T(8,128)(2,1)S(1)} %attend_finish.1), channel_id=1, replica_groups=mesh['grp'=2,'blk'=4,'head'=4] {'blk','head':(1)2}, dimensions={0} | all-to-all | bytes 393216 | tf_op jit(solution)/shard_map/all_to_all | solution.py:337
  33.5 0.9 %unpack_heads.1 = (f32[64,512]{1,0:T(8,128)}, f32[64,512]{1,0:T(8,128)}, f32[64,512]{1,0:T(8,128)}) custom-call(bf16[8,96,128]{2,1,0:T(8,128)(2,1)S(1)} %all_to_all.11.in_ref), custom_call_target="tpu_custom_call" | custom-call | tf_op jit(solution)/shard_map/unpack_heads/pallas_call | solution.py:317
Async XLA Ops:
  1.7 16.1 %copy-start = (s32[32]{0:T(128)S(1)}, s32[32]{0:T(128)}, u32[]{:S(2)}) copy-start(s32[32]{0:T(128)} %valid_ref.1) | copy-start | bytes 388
  1.7 16.1 %copy-start.1 = (s32[32]{0:T(128)S(1)}, s32[32]{0:T(128)}, u32[]{:S(2)}) copy-start(s32[32]{0:T(128)} %views_ref.1) | copy-start | bytes 388
  1.7 16.1 %copy-start.2 = (f32[8]{0:T(128)S(1)}, f32[8]{0:T(128)}, u32[]{:S(2)}) copy-start(f32[8]{0:T(128)} %bias_ref.1) | copy-start | bytes 100
  17.8 1.5 %collective-permute-start = (bf16[8,128,128]{2,1,0:T(8,128)(2,1)S(1)}, bf16[8,128,128]{2,1,0:T(8,128)(2,1)S(1)}, u32[]{:S(2)}, u32[]{:S(2)}) collective-permute-start(bf16[8,128,128]{2,1,0:T(8,128)(2,1)S(1)} %all_to_all.10.mine_ref.refs_0_), channel_id=1, source_target_pairs={{1,0},{0,1},{3,2},{2,3},{5,4},{4,5},{7,6},{6,7},{9,8},{8,9},{11,10... | collective-permute-start | bytes 786440 | tf_op jit(solution)/shard_map/ppermute | solution.py:333

commit v15 on v9

--- a/solution.py
+++ b/solution.py
@@ -159,7 +159,8 @@
             there = slice((block - 1) * own, block * own)
             flip_ref[:, here] = kv.astype(jnp.float32).T[:HD].astype(jnp.bfloat16)
             qg_ref[there, :] = blocks[block][:, rows:, :].reshape(own, PAIR)
-    sum_ref[...] = jnp.zeros_like(sum_ref)
+    if shares > 2:
+        sum_ref[...] = jnp.zeros_like(sum_ref)
 
     def score(ours, index):
         if ours:
@@ -210,14 +211,15 @@
                 lows.append(weight.reshape(CHUNK, TILE).astype(jnp.bfloat16))
         return jnp.concatenate(grads, axis=0), jnp.concatenate(lows, axis=0)
 
-    def leave(ours, first, pair):
+    def leave(ours, first, pair, fresh):
         weights, grads, lows = zip(*pair)
         factors = [x for both in zip(grads, lows) for x in (both[0][:own], both[1])]
-        sum_ref[...] += jnp.dot(
+        added = jnp.dot(
             jnp.concatenate(factors, axis=1),
             jnp.concatenate([each[:, :PAIR] for each in weights], axis=0),
             preferred_element_type=jnp.float32,
         )
+        sum_ref[...] = added if fresh else sum_ref[...] + added
         if ours:
             turned = jnp.dot(
                 flip_ref[...], side_by_side(*grads), preferred_element_type=jnp.float32
@@ -237,7 +239,8 @@
                 weights, parts = expos.pop(step - 2)
                 done[step - 2] = (weights, *gradients(*work[step - 2], parts))
                 if step % 2:
-                    leave(*work[step - 3], (done.pop(step - 3), done.pop(step - 2)))
+                    pair = (done.pop(step - 3), done.pop(step - 2))
+                    leave(*work[step - 3], pair, step == 3 and shares <= 2)
 
     others = tiles * (shares - 1)
     if shares <= 2:

time: 34.3 us -> 34.3 us (level)
  no operation moved by 1% of the time
where the time goes in v15:
time: 34.3 us; the launch traced here: 34.1 us
  blocking collectives  27.8 us (81%)
  Pallas kernels  5.29 us (15%)
  between operations  0.68 us (2%)
    all_to_all x1, blocking collectives, local(): mine = swap(pack(query, keys, values, grad_out))  16.1 us
    all_to_all x1, blocking collectives, local(): return unpack(swap(given), query.shape[0])  11.7 us
    pallas_call x1, Pallas kernels, attend(): pl.pallas_call(functools.partial(finish_kernel, shares), out_shape=pltpu....  2.17 us
    pallas_call x1, Pallas kernels, attend(): pl.pallas_call(functools.partial(begin_kernel, shares), out_shape=(pltpu....  1.19 us
    pallas_call x1, Pallas kernels, pack(): pl.pallas_call(pack_kernel, out_shape=pltpu.VMEM((width // HD, 2 * rows,...  1.07 us
    pallas_call x1, Pallas kernels, unpack(): pl.pallas_call(unpack_kernel, out_shape=(shape,) * 3, in_specs=[VMEM], ou...  0.85 us
  transfers between devices with their start and end apart: 1, of which 1 were waited for; matrix products, arithmetic and copies ran while one was open for 0% of the time, Pallas kernels for 4%

profile of v15, /device:TPU:0, one launch (start us, length us, event | category | flops | bytes accessed | tf_op | source)
XLA Modules:
  0.0 34.1 jit_solution(12611299109953840858)
XLA Ops:
  0.6 1.1 %pack_heads.1 = bf16[8,128,128]{2,1,0:T(8,128)(2,1)S(1)} custom-call(bf16[64,512]{1,0:T(8,128)(2,1)} %q_ref.1, bf16[64,512]{1,0:T(8,128)(2,1)} %k_ref.1, bf16[64,512]{1,0:T(8,128)(2,1)} %v_ref.1, bf16[64,512]{1,0:T(8,128)(2,1)} %g_ref.1), custom_call_target="tpu_custom_call" | custom-call | tf_op jit(solution)/shard_map/pack_heads/pallas_call | solution.py:42
  1.7 0.0 copy-start
  1.7 0.0 copy-start.1
  1.7 0.0 copy-start.2
  1.7 16.1 %all_to_all.10.mine_ref.refs_0_ = bf16[8,128,128]{2,1,0:T(8,128)(2,1)S(1)} all-to-all(bf16[8,128,128]{2,1,0:T(8,128)(2,1)S(1)} %pack_heads.1), channel_id=1, replica_groups=mesh['grp'=2,'blk'=4,'head'=4] {'blk','head':(1)2}, dimensions={0} | all-to-all | bytes 524288 | tf_op jit(solution)/shard_map/all_to_all | solution.py:334
  17.8 0.0 collective-permute-start
  17.8 0.0 copy-done
  17.8 0.0 copy-done.1
  17.9 0.0 copy-done.2
  17.9 1.2 %attend_begin.1 = (bf16[1024,128]{1,0:T(8,128)(2,1)S(1)}, bf16[1024,128]{1,0:T(8,128)(2,1)S(1)}, bf16[4,256,256]{2,1,0:T(8,128)(2,1)S(1)}, bf16[64,512]{1,0:T(8,...) custom-call(bf16[8,128,128]{2,1,0:T(8,128)(2,1)S(1)} %all_to_all.10.mine_ref, ...), custom_call_target="tpu_custom_call" | custom-call | flops 268435456 | bytes 2097152 | tf_op jit(solution)/shard_map/attend_begin/pallas_call | solution.py:267
  19.1 0.3 collective-permute-done.refs_1_
  19.4 2.2 %attend_finish.1 = bf16[8,96,128]{2,1,0:T(8,128)(2,1)S(1)} custom-call(bf16[8,128,128]{2,1,0:T(8,128)(2,1)S(1)} %all_to_all.10.mine_ref.refs_0_, bf16[8,128,128]{2,1,0:T(8,128)(2,1)S(1)} %collective-permute-done.refs_1_, bf16[1024,128]{1,0:T(8,128)(2,1)S(1)} %get-tuple-element.10.refs_2_, bf16[1024,128]{1,0:T(8,128)(2,1)S(1)} %get-tuple-element.11.refs_3_, ...), custom_call_target="tpu_custom_call" | custom-call | tf_op jit(solution)/shard_map/attend_finish/pallas_call | solution.py:287
  21.5 11.7 %all_to_all.11.in_ref = bf16[8,96,128]{2,1,0:T(8,128)(2,1)S(1)} all-to-all(bf16[8,96,128]{2,1,0:T(8,128)(2,1)S(1)} %attend_finish.1), channel_id=1, replica_groups=mesh['grp'=2,'blk'=4,'head'=4] {'blk','head':(1)2}, dimensions={0} | all-to-all | bytes 393216 | tf_op jit(solution)/shard_map/all_to_all | solution.py:340
  33.2 0.9 %unpack_heads.1 = (f32[64,512]{1,0:T(8,128)}, f32[64,512]{1,0:T(8,128)}, f32[64,512]{1,0:T(8,128)}) custom-call(bf16[8,96,128]{2,1,0:T(8,128)(2,1)S(1)} %all_to_all.11.in_ref), custom_call_target="tpu_custom_call" | custom-call | tf_op jit(solution)/shard_map/unpack_heads/pallas_call | solution.py:320
Async XLA Ops:
  1.7 16.1 %copy-start = (s32[32]{0:T(128)S(1)}, s32[32]{0:T(128)}, u32[]{:S(2)}) copy-start(s32[32]{0:T(128)} %valid_ref.1) | copy-start | bytes 388
  1.7 16.1 %copy-start.1 = (s32[32]{0:T(128)S(1)}, s32[32]{0:T(128)}, u32[]{:S(2)}) copy-start(s32[32]{0:T(128)} %views_ref.1) | copy-start | bytes 388
  1.7 16.1 %copy-start.2 = (f32[8]{0:T(128)S(1)}, f32[8]{0:T(128)}, u32[]{:S(2)}) copy-start(f32[8]{0:T(128)} %bias_ref.1) | copy-start | bytes 100
  17.8 1.5 %collective-permute-start = (bf16[8,128,128]{2,1,0:T(8,128)(2,1)S(1)}, bf16[8,128,128]{2,1,0:T(8,128)(2,1)S(1)}, u32[]{:S(2)}, u32[]{:S(2)}) collective-permute-start(bf16[8,128,128]{2,1,0:T(8,128)(2,1)S(1)} %all_to_all.10.mine_ref.refs_0_), channel_id=1, source_target_pairs={{1,0},{0,1},{3,2},{2,3},{5,4},{4,5},{7,6},{6,7},{9,8},{8,9},{11,10... | collective-permute-start | bytes 786440 | tf_op jit(solution)/shard_map/ppermute | solution.py:336
